TPU v7x, 128 devices: a whole 4x4x4 slice. The times are simulated.
128 devices in a mesh: dp: 16 (over z, y_lo, core), fsdp: 8 (over x, y_hi).
Axes of the slice: x: 4, y: 4 (y_hi: 2, y_lo: 2; y = y_hi * 2 + y_lo), z: 4, core: 2. Of those that a mesh axis runs over, the one named last changes fastest.
Arguments:
- pooled: bfloat16 [16384, 1152], P(('dp', 'fsdp')), may hold values from -6 to 6
- text_feats: bfloat16 [16384, 1152], P(('dp', 'fsdp')), may hold values from -6 to 6
- out_weight: bfloat16 [1152, 1152], P('fsdp'), may hold values from -0.1875 to 0.1875
- logit_scale: float32 [1], replicated, may hold values from 8 to 12
- logit_bias: float32 [1], replicated, may hold values from -7 to -4
Outputs:
- grad_text: float32 [16384, 1152], P(('dp', 'fsdp'))
- grad_pooled: bfloat16 [16384, 1152], P(('dp', 'fsdp'))
- grad_weight: float32 [1152, 1152], P('fsdp')
All inputs are finite; a program needn't handle non-finite values.
Results may differ from a plain program's by a relative error of at most 0.028.
Values may be sent and summed in bfloat16 or wider, within the bound.
No kernel may reach another device: no remote copies, remote signals or barrier semaphores. Data moves between devices by JAX's collectives and lax.ppermute only.
A program may use at most 128 MiB of HBM per device.

v0:
```python
import functools

import jax
import jax.numpy as jnp
from jax import lax
from jax.experimental import pallas as pl
from jax.experimental.pallas import tpu as pltpu
from jax.sharding import PartitionSpec as P

epsilon = 1e-06
BF = jnp.bfloat16
F32 = jnp.float32
AXES = ("dp", "fsdp")
SIZES = {"z": 4, "yl": 2, "c": 2, "x": 4, "yh": 2}


def place_of(i):
    dp, fs = divmod(i, 8)
    return {"z": dp // 4, "yl": dp // 2 % 2, "c": dp % 2, "x": fs // 2, "yh": fs % 2}


def index_of(p):
    return (p["z"] * 4 + p["yl"] * 2 + p["c"]) * 8 + p["x"] * 2 + p["yh"]


def shift(value, axis, by):
    pairs = []
    for i in range(128):
        p = place_of(i)
        p[axis] = (p[axis] + by) % SIZES[axis]
        pairs.append((i, index_of(p)))
    return lax.ppermute(value, AXES, pairs)


def join(*values):
    return lax.optimization_barrier(values)


def both_ways(block, axis):
    return shift(block, axis, -1), shift(block, axis, 1)


def rows_of(v, k, n=128):
    return v[k * n:(k + 1) * n]


def ring_first(v, axis):
    half = v[0].shape[0] // 2
    far = v[2].astype(BF)
    a = shift(far[:half], axis, 1).astype(F32)
    b = shift(far[half:], axis, -1).astype(F32)
    plus = jnp.concatenate([v[1][:half] + a, v[1][half:]], 0).astype(BF)
    minus = jnp.concatenate([v[3][:half], v[3][half:] + b], 0).astype(BF)
    return v[0], plus, minus


def ring_second(own, plus, minus, axis):
    return own + (shift(plus, axis, 1).astype(F32) + shift(minus, axis, -1).astype(F32))


def near_sum(v, axis, n=128):
    r1 = shift(rows_of(v, 1, n), axis, 1).astype(F32)
    r2 = shift(rows_of(v, 2, n), axis, 2).astype(F32)
    r3 = shift(rows_of(v, 3, n), axis, -1).astype(F32)
    return (rows_of(v, 0, n).astype(F32) + r2) + (r1 + r3)


def unit_rows(values):
    norms = jnp.sqrt(jnp.sum(values * values, axis=-1, keepdims=True) + epsilon)
    return (values / norms, norms)


def unit_backward(upstream, unit, norms):
    return (upstream - unit * jnp.sum(unit * upstream, axis=-1, keepdims=True)) / norms


def block_row(pos, dx, dy):
    x, yh = pos[0], pos[1]
    return (lax.rem(x + dx, 4) * 2 + lax.rem(yh + dy, 2)) * 144


def prepare_kernel(pos, weight, pooled, text, own, emb):
    own[pl.ds(0, 80), :] = weight[pl.ds(pl.multiple_of(pos[2] * 64, 16), 80), :]
    own[pl.ds(80, 128), :] = pooled[...]
    values = text[...].astype(F32)
    emb[...] = (values / jnp.sqrt(jnp.sum(values * values, axis=-1, keepdims=True) + epsilon)).astype(BF)


def prepare(pos, weight, pooled, text):
    return pl.pallas_call(
        prepare_kernel,
        out_shape=[jax.ShapeDtypeStruct((208, 1152), BF), jax.ShapeDtypeStruct((128, 1152), BF)],
        in_specs=[pl.BlockSpec(memory_space=pltpu.SMEM)] + [pl.BlockSpec(memory_space=pltpu.VMEM)] * 3,
        out_specs=[pl.BlockSpec(memory_space=pltpu.VMEM)] * 2,
        compiler_params=pltpu.CompilerParams(vmem_limit_bytes=32 * 2**20),
    )(pos, weight, pooled, text)


def assemble_kernel(pos, near, far, near_c, far_c, out):
    c = pos[2]
    for dx in range(4):
        for dy in range(2):
            own, oth, k = (far, far_c, 96 * dy) if dx == 2 else (near, near_c, ((0, 1, 2, 2)[dx] * 2 + dy) * 80)
            base = block_row(pos, dx, dy)
            out[pl.ds(pl.multiple_of(base + c * 64, 16), 80), :] = own[pl.ds(k, 80), :]
            out[pl.ds(pl.multiple_of(base + 80 * (1 - c), 16), 64), :] = oth[pl.ds(pl.multiple_of(k + 16 * (1 - c), 16), 64), :]


def assemble(pos, *parts):
    return pl.pallas_call(
        assemble_kernel,
        out_shape=jax.ShapeDtypeStruct((1152, 1152), BF),
        in_specs=[pl.BlockSpec(memory_space=pltpu.SMEM)] + [pl.BlockSpec(memory_space=pltpu.VMEM)] * 4,
        out_specs=pl.BlockSpec(memory_space=pltpu.VMEM),
        compiler_params=pltpu.CompilerParams(vmem_limit_bytes=32 * 2**20),
    )(pos, *parts)


def spread_kernel(pos, whole, keep, send):
    c = pos[2]
    for dx in range(4):
        for dy in range(2):
            k = dx * 2 + dy
            base = block_row(pos, dx, dy)
            keep[pl.ds(k * 80, 80), :] = whole[pl.ds(pl.multiple_of(base + c * 64, 16), 80), :]
            send[pl.ds(k * 80, 80), :] = whole[pl.ds(pl.multiple_of(base + (1 - c) * 64, 16), 80), :]


def spread(pos, whole):
    return pl.pallas_call(
        spread_kernel,
        out_shape=[jax.ShapeDtypeStruct((640, 1152), BF)] * 2,
        in_specs=[pl.BlockSpec(memory_space=pltpu.SMEM), pl.BlockSpec(memory_space=pltpu.VMEM)],
        out_specs=[pl.BlockSpec(memory_space=pltpu.VMEM)] * 2,
        compiler_params=pltpu.CompilerParams(vmem_limit_bytes=32 * 2**20),
    )(pos, whole)


def local(pooled, text_feats, out_weight, logit_scale, logit_bias):
    dp = lax.axis_index("dp")
    fs = lax.axis_index("fsdp")
    core = dp % 2
    pos = jnp.stack([fs // 2, fs % 2, core]).astype(jnp.int32)
    mult = logit_scale[0]
    bias = logit_bias[0]

    own, text_emb = prepare(pos, out_weight, pooled, text_feats)
    oth = shift(own, "yh", 1)
    own_p, own_m = both_ways(own, "x")
    oth_p, oth_m = both_ways(oth, "x")
    far_a = shift(jnp.concatenate([own_m[:96], oth_m[:96]], 0), "x", 1)
    far_b = shift(jnp.concatenate([own_p[96:], oth_p[96:]], 0), "x", -1)
    w_near = jnp.concatenate([v[:80] for v in (own, oth, own_p, oth_p, own_m, oth_m)], 0)
    w_far_c = shift(far_a, "c", 1)
    weight = assemble(pos, w_near, far_a, shift(w_near, "c", 1), w_far_c)
    images = jnp.concatenate([
        pooled, own_p[80:], far_a[80:96], far_b[:112], own_m[80:],
        oth[80:], oth_p[80:], far_a[176:], far_b[112:], oth_m[80:]], 0)

    text_own, _ = join(text_emb, oth)
    text_oth = shift(text_own, "yl", 1)
    t_p, t_m = both_ways(text_emb, "z")
    u_p, u_m = both_ways(text_oth, "z")
    fa = shift(jnp.concatenate([t_m[:64], u_m[:64]], 0), "z", 1)
    fb = shift(jnp.concatenate([t_p[64:], u_p[64:]], 0), "z", -1)
    t_near = jnp.concatenate([text_emb, text_oth, t_p, u_p, t_m, u_m], 0)
    t_far = jnp.concatenate([fa[:64], fb[:64], fa[64:], fb[64:]], 0)
    t_near, t_far, _ = join(t_near, t_far, w_far_c)
    c_near = shift(t_near, "c", 1)
    c_far = shift(t_far, "c", 1)
    texts = jnp.concatenate([t_near[:512], t_far, t_near[512:], c_near[:512], c_far, c_near[512:]], 0)

    def embed(rows):
        raw = jnp.dot(rows, weight, preferred_element_type=F32)
        unit, norm = unit_rows(raw)
        return unit.astype(BF), norm

    emb, norm = embed(images)

    def pair(e, t):
        logits = mult * lax.dot_general(e, t, (((1,), (1,)), ((), ())), preferred_element_type=F32) + bias
        return (jax.nn.sigmoid(logits) * mult).astype(BF)

    def pair_own(e, t):
        logits = mult * lax.dot_general(e, t, (((1,), (1,)), ((), ())), preferred_element_type=F32) + bias
        row = lax.broadcasted_iota(jnp.int32, logits.shape, 0)
        col = lax.broadcasted_iota(jnp.int32, logits.shape, 1)
        sign = jnp.where(row == col, 1.0, -1.0)
        return (-sign * jax.nn.sigmoid(-sign * logits) * mult).astype(BF)

    def back_t(pg, e):
        return lax.dot_general(pg, e, (((0,), (0,)), ((), ())), preferred_element_type=F32)

    def project(g, e, n):
        return unit_backward(g, e.astype(F32), n)

    grads = lax.dynamic_update_slice(pair(emb, texts), pair_own(emb[:128], texts[:128]), (0, 0))
    r0 = project(jnp.dot(grads[:512], texts, preferred_element_type=F32), emb[:512], norm[:512]).astype(BF)
    r1 = project(jnp.dot(grads[512:], texts, preferred_element_type=F32), emb[512:], norm[512:]).astype(BF)

    r1_here = shift(r1, "yh", 1)
    gw = (back_t(images[:512], r0) + back_t(images[512:], r1)).astype(BF)
    keep, send = spread(pos, gw)
    send = shift(send, "c", 1)
    gt_send = back_t(grads[:, 1024:], emb)
    keep, send, gt_send = join(keep, send, gt_send)
    gt_send = gt_send.astype(BF)

    s, grads = join((keep.astype(F32) + send.astype(F32)).astype(BF), grads)
    s = near_sum(s, "x", 160)
    gt = back_t(grads[:, :1024], emb)
    gt = gt + shift(gt_send, "c", 1).astype(F32)
    gt = ring_first([rows_of(gt, k, 256) for k in range(4)], "z")
    s, gt, r0 = join(s, gt, r0)

    s = (s[:80] + shift(s[80:].astype(BF), "yh", 1).astype(F32)).astype(BF)
    s = (s.astype(F32) + shift(s, "yl", 1).astype(F32)).astype(BF)
    gt = ring_second(*gt, "z")
    r0 = r0.astype(F32) + r1_here.astype(F32)
    raw_grad = near_sum(r0.astype(BF), "x").astype(BF)
    gt, gt_y, s, raw_grad = join(gt[:128], gt[128:].astype(BF), s, raw_grad)

    text_grad = gt + shift(gt_y, "yl", 1).astype(F32)
    text_unit, text_norm = unit_rows(text_feats.astype(F32))
    grad_text = unit_backward(text_grad, text_unit, text_norm)
    zp, zm, zf = shift(s, "z", 1), shift(s, "z", -1), shift(s, "z", 2)
    s = ((s.astype(F32) + zf.astype(F32)) + (zp.astype(F32) + zm.astype(F32))).astype(BF)
    o = shift(s, "c", 1)
    lo = jnp.where(core == 0, s, o)
    hi = jnp.where(core == 0, o, s)
    grad_weight = jnp.concatenate([lo, hi[16:]], 0).astype(F32)
    grad_pooled = lax.dot_general(raw_grad, weight, (((1,), (1,)), ((), ())), preferred_element_type=F32).astype(BF)
    return (grad_text, grad_pooled, grad_weight)


def solution(mesh):
    placed = (P(AXES, None), P(AXES, None), P("fsdp", None), P(), P())
    return jax.shard_map(
        local,
        mesh=mesh,
        in_specs=placed,
        out_specs=(P(AXES, None), P(AXES, None), P("fsdp", None)),
        check_vma=False,
    )
```

profile of v0, /device:TPU:1, one launch (start us, length us, event | category | flops | bytes accessed | tf_op | source)
XLA Modules:
  0.0 158.1 jit_solution(5992891153509903978)
XLA Ops:
  4.3 3.8 %collective-permute-start.2 = (bf16[208,1152]{1,0:T(8,128)(2,1)S(1)}, bf16[208,1152]{1,0:T(8,128)(2,1)S(1)}, u32[]{:S(2)}, u32[]{:S(2)}) collective-permute-start(bf16[208,1152]{1,0:T(8,128)(2,1)S(1)} %get-tuple-element.24), channel_id=1, source_target_pairs={{0,1},{1,0},{2,3},{3,2},{4,5},{5,4},{6,7},{7,6},{8,9},{9,8},{10,11... | collective-permute-start | bytes 1437704 | tf_op jit(solution)/shard_map/ppermute | solution.py:32
  9.4 1.5 collective-permute-start
  10.8 3.8 %collective-permute-start.10 = (bf16[128,1152]{1,0:T(8,128)(2,1)S(1)}, bf16[128,1152]{1,0:T(8,128)(2,1)S(1)}, u32[]{:S(2)}, u32[]{:S(2)}) collective-permute-start(bf16[128,1152]{1,0:T(8,128)(2,1)S(1)} %get-tuple-element.26), channel_id=1, source_target_pairs={{0,96},{1,97},{2,98},{3,99},{4,100},{5,101},{6,102},{7,103},{8,104... | collective-permute-start | bytes 884744 | tf_op jit(solution)/shard_map/ppermute | solution.py:32
  16.0 3.4 %collective-permute-done.10 = bf16[128,1152]{1,0:T(8,128)(2,1)S(1)} collective-permute-done((bf16[128,1152]{1,0:T(8,128)(2,1)S(1)}, bf16[128,1152]{1,0:T(8,128)(2,1)S(1)}, u32[]{:S(2)}, u32[]{:S(2)}) %collective-permute-start.10) | collective-permute-done | bytes 294944 | tf_op jit(solution)/shard_map/ppermute | solution.py:32
  19.4 3.1 %collective-permute-done.12 = bf16[128,1152]{1,0:T(8,128)(2,1)S(1)} collective-permute-done((bf16[128,1152]{1,0:T(8,128)(2,1)S(1)}, bf16[128,1152]{1,0:T(8,128)(2,1)S(1)}, u32[]{:S(2)}, u32[]{:S(2)}) %collective-permute-start.12) | collective-permute-done | bytes 294944 | tf_op jit(solution)/shard_map/ppermute | solution.py:32
  24.6 3.5 %collective-permute-done.9 = bf16[128,1152]{1,0:T(8,128)(2,1)S(1)} collective-permute-done((bf16[128,1152]{1,0:T(8,128)(2,1)S(1)}, bf16[128,1152]{1,0:T(8,128)(2,1)S(1)}, u32[]{:S(2)}, u32[]{:S(2)}) %collective-permute-start.9) | collective-permute-done | bytes 294944 | tf_op jit(solution)/shard_map/ppermute | solution.py:32
  29.6 4.9 %collective-permute-done.3 = bf16[208,1152]{1,0:T(8,128)(2,1)S(1)} collective-permute-done((bf16[208,1152]{1,0:T(8,128)(2,1)S(1)}, bf16[208,1152]{1,0:T(8,128)(2,1)S(1)}, u32[]{:S(2)}, u32[]{:S(2)}) %collective-permute-start.3) | collective-permute-done | bytes 479264 | tf_op jit(solution)/shard_map/ppermute | solution.py:32
  34.8 2.7 %collective-permute-start.6 = (bf16[224,1152]{1,0:T(8,128)(2,1)S(1)}, bf16[224,1152]{1,0:T(8,128)(2,1)S(1)}, u32[]{:S(2)}, u32[]{:S(2)}) collective-permute-start(bf16[224,1152]{1,0:T(8,128)(2,1)S(1)} %pad_maximum_fusion.3), channel_id=1, source_target_pairs={{0,6},{1,7},{2,0},{3,1},{4,2},{5,3},{6,4},{7,5},{8,14},{9,15},{10,... | collective-permute-start | bytes 1548296 | tf_op jit(solution)/shard_map/ppermute | solution.py:32
  37.6 4.8 %collective-permute-start.7 = (bf16[480,1152]{1,0:T(8,128)(2,1)S(1)}, bf16[480,1152]{1,0:T(8,128)(2,1)S(1)}, u32[]{:S(2)}, u32[]{:S(2)}) collective-permute-start(bf16[480,1152]{1,0:T(8,128)(2,1)S(1)} %slice_dynamic-update-slice_fusion.18.near), channel_id=1, source_target_pairs={{0,8},{1,9},{2,10},{3,11},{4,12},{5,13},{6,14},{7,15},{8,0},{9,1},... | collective-permute-start | bytes 3317768 | tf_op jit(solution)/shard_map/ppermute | solution.py:32
  42.6 2.0 %collective-permute-start.15 = (bf16[128,1152]{1,0:T(8,128)(2,1)S(1)}, bf16[128,1152]{1,0:T(8,128)(2,1)S(1)}, u32[]{:S(2)}, u32[]{:S(2)}) collective-permute-start(bf16[128,1152]{1,0:T(8,128)(2,1)S(1)} %pad_maximum_fusion.6), channel_id=1, source_target_pairs={{0,96},{1,97},{2,98},{3,99},{4,100},{5,101},{6,102},{7,103},{8,104... | collective-permute-start | bytes 884744 | tf_op jit(solution)/shard_map/ppermute | solution.py:32
  44.9 6.4 %collective-permute-done.15 = bf16[128,1152]{1,0:T(8,128)(2,1)S(1)} collective-permute-done((bf16[128,1152]{1,0:T(8,128)(2,1)S(1)}, bf16[128,1152]{1,0:T(8,128)(2,1)S(1)}, u32[]{:S(2)}, u32[]{:S(2)}) %collective-permute-start.15) | collective-permute-done | bytes 294944 | tf_op jit(solution)/shard_map/ppermute | solution.py:32
  51.3 2.9 %collective-permute-done.14 = bf16[128,1152]{1,0:T(8,128)(2,1)S(1)} collective-permute-done((bf16[128,1152]{1,0:T(8,128)(2,1)S(1)}, bf16[128,1152]{1,0:T(8,128)(2,1)S(1)}, u32[]{:S(2)}, u32[]{:S(2)}) %collective-permute-start.14) | collective-permute-done | bytes 294944 | tf_op jit(solution)/shard_map/ppermute | solution.py:32
  58.5 3.6 %multiply_reduce_fusion = (f32[1024]{0:T(1024)S(1)}, f32[1024,1152]{1,0:T(8,128)S(1)}) fusion(bf16[1024,1152]{1,0:T(8,128)(2,1)S(1)} %get-tuple-element.67, bf16[1152,1152]{1,0:T(8,128)(2,1)S(1)} %shard_map.77), kind=kOutput, calls=%fused_computation.5 | convolution fusion | flops 2720267264 | bytes 9736192 | tf_op jit(solution)/shard_map/dot_general | solution.py:174
  63.0 6.9 %multiply_convert_fusion = bf16[1024,2048]{1,0:T(8,128)(2,1)S(1)} fusion(bf16[1024,1152]{1,0:T(8,128)(2,1)S(1)} %divide_convert_fusion, bf16[2048,1152]{1,0:T(8,128)(2,1)S(1)} %slice_dynamic-update-slice_fusion.2, f32[]{:T(128)} %bitcast.21, f32[]{:T(128)} %bitcast.19), kind=kOutput, calls=%fused_computation.1 | convolution fusion | flops 4846518272 | bytes 11272200 | tf_op jit(solution)/shard_map/dot_general | solution.py:181
  70.2 2.9 %fusion.13 = f32[512,1152]{1,0:T(8,128)S(1)} fusion(bf16[2048,1152]{1,0:T(8,128)(2,1)S(1)} %slice_dynamic-update-slice_fusion.2, bf16[1024,2048]{1,0:T(8,128)(2,1)S(1)} %fusion.26), kind=kOutput, calls=%fused_computation.25 | convolution fusion | flops 2415919104 | bytes 9175040 | tf_op jit(solution)/shard_map/dot_general | solution.py:198
  73.1 3.2 %fusion.5 = (f32[512]{0:T(512)S(1)}, f32[512]{0:T(512)S(1)}, f32[512,1152]{1,0:T(8,128)S(1)}) fusion(bf16[1024,1152]{1,0:T(8,128)(2,1)S(1)} %divide_convert_fusion, f32[512,1152]{1,0:T(8,128)S(1)} %fusion.13, bf16[2048,1152]{1,0:T(8,128)(2,1)S(1)} %slice_dynamic-update-slice_fusion.2, bf16[1024,2048]{1,0:T(8,128)(2,1)S(1)} %fusion.26), kind=kOutput, calls=%fused_computation.16 | convolution fusion | flops 2419457024 | bytes 13897728 | tf_op jit(solution)/shard_map/dot_general | solution.py:199
  77.3 1.7 %fusion.39 = f32[1152,1152]{1,0:T(8,128)S(1)} fusion(bf16[512,1152]{1,0:T(8,128)(2,1)S(1)} %get-tuple-element.69, bf16[512,1152]{1,0:T(8,128)(2,1)S(1)} %get-tuple-element.40), kind=kOutput, calls=%fused_computation.119 | convolution fusion | flops 1358954496 | bytes 7667712 | tf_op jit(solution)/shard_map/dot_general | solution.py:192
  79.1 1.7 %fusion.whole = bf16[1152,1152]{1,0:T(8,128)(2,1)S(1)} fusion(f32[1152,1152]{1,0:T(8,128)S(1)} %fusion.39, bf16[512,1152]{1,0:T(8,128)(2,1)S(1)} %get-tuple-element.66, bf16[512,1152]{1,0:T(8,128)(2,1)S(1)} %get-tuple-element.55), kind=kOutput, calls=%fused_computation.2 | convolution fusion | flops 1361608704 | bytes 10321920 | tf_op jit(solution)/shard_map/dot_general | solution.py:192
  82.1 14.2 %fusion.9 = bf16[1024,1152]{1,0:T(8,128)(2,1)} fusion(bf16[1024,1152]{1,0:T(8,128)(2,1)S(1)} %divide_convert_fusion, bf16[1024,2048]{1,0:T(8,128)(2,1)S(1)} %fusion.26), kind=kOutput, calls=%fused_computation.21 | convolution fusion | flops 2415919104 | bytes 6815744 | tf_op jit(solution)/shard_map/dot_general | solution.py:192
  97.9 2.7 %collective-permute-start.29 = (bf16[512,1152]{1,0:T(8,128)(2,1)}, bf16[512,1152]{1,0:T(8,128)(2,1)S(1)}, u32[]{:S(2)}, u32[]{:S(2)}) collective-permute-start(bf16[512,1152]{1,0:T(8,128)(2,1)} %copy-done.9), channel_id=1, source_target_pairs={{0,1},{1,0},{2,3},{3,2},{4,5},{5,4},{6,7},{7,6},{8,9},{9,8},{10,11... | collective-permute-start | bytes 3538952 | tf_op jit(solution)/shard_map/ppermute | solution.py:32
  100.6 2.2 %add_convert_fusion = bf16[640,1152]{1,0:T(8,128)(2,1)S(1)} fusion(bf16[640,1152]{1,0:T(8,128)(2,1)} %copy-done.10, bf16[640,1152]{1,0:T(8,128)(2,1)} %copy-done.2), kind=kLoop, calls=%fused_computation.6 | loop fusion | flops 2949120 | bytes 4423680 | tf_op jit(solution)/shard_map/convert_element_type | solution.py:209
  104.4 3.0 %fusion.15 = f32[1024,1152]{1,0:T(8,128)S(1)} fusion(bf16[1024,1152]{1,0:T(8,128)(2,1)S(1)} %copy-done.8, bf16[1024,2048]{1,0:T(8,128)(2,1)S(1)} %copy-done.15), kind=kOutput, calls=%fused_computation.27 | convolution fusion | flops 2415919104 | bytes 9175040 | tf_op jit(solution)/shard_map/dot_general | solution.py:192
  107.4 2.4 %fusion.32 = (bf16[1024,1152]{1,0:T(8,128)(2,1)S(1)}, f32[1024,1152]{1,0:T(8,128)S(1)}) fusion(f32[1024,1152]{1,0:T(8,128)S(1)} %fusion.15, bf16[1024,1152]{1,0:T(8,128)(2,1)} %collective-permute-done.22), kind=kLoop, calls=%fused_computation.112 | loop fusion | flops 3538944 | bytes 14155776 | tf_op jit(solution)/shard_map/convert.8
  110.0 2.6 %collective-permute-done.21 = bf16[160,1152]{1,0:T(8,128)(2,1)S(1)} collective-permute-done((bf16[160,1152]{1,0:T(8,128)(2,1)S(1)}, bf16[160,1152]{1,0:T(8,128)(2,1)S(1)}, u32[]{:S(2)}, u32[]{:S(2)}) %collective-permute-start.21) | collective-permute-done | bytes 368672 | tf_op jit(solution)/shard_map/ppermute | solution.py:32
  112.6 9.2 %collective-permute-done.20 = bf16[160,1152]{1,0:T(8,128)(2,1)S(1)} collective-permute-done((bf16[160,1152]{1,0:T(8,128)(2,1)S(1)}, bf16[160,1152]{1,0:T(8,128)(2,1)S(1)}, u32[]{:S(2)}, u32[]{:S(2)}) %collective-permute-start.20) | collective-permute-done | bytes 368672 | tf_op jit(solution)/shard_map/ppermute | solution.py:32
  124.4 2.6 %collective-permute-done.29 = bf16[512,1152]{1,0:T(8,128)(2,1)S(1)} collective-permute-done((bf16[512,1152]{1,0:T(8,128)(2,1)}, bf16[512,1152]{1,0:T(8,128)(2,1)S(1)}, u32[]{:S(2)}, u32[]{:S(2)}) %collective-permute-start.29) | collective-permute-done | bytes 1179680 | tf_op jit(solution)/shard_map/ppermute | solution.py:32
  131.2 3.7 %collective-permute-done.32 = bf16[128,1152]{1,0:T(8,128)(2,1)S(1)} collective-permute-done((bf16[128,1152]{1,0:T(8,128)(2,1)S(1)}, bf16[128,1152]{1,0:T(8,128)(2,1)S(1)}, u32[]{:S(2)}, u32[]{:S(2)}) %collective-permute-start.32) | collective-permute-done | bytes 294944 | tf_op jit(solution)/shard_map/ppermute | solution.py:32
  135.1 7.4 %collective-permute-done.31 = bf16[128,1152]{1,0:T(8,128)(2,1)S(1)} collective-permute-done((bf16[128,1152]{1,0:T(8,128)(2,1)S(1)}, bf16[128,1152]{1,0:T(8,128)(2,1)S(1)}, u32[]{:S(2)}, u32[]{:S(2)}) %collective-permute-start.31) | collective-permute-done | bytes 294944 | tf_op jit(solution)/shard_map/ppermute | solution.py:32
  144.6 1.6 %convolution_convert_fusion = bf16[128,1152]{1,0:T(8,128)(2,1)} fusion(bf16[128,1152]{1,0:T(8,128)(2,1)S(1)} %add_convert_fusion.2, bf16[1152,1152]{1,0:T(8,128)(2,1)S(1)} %shard_map.77), kind=kOutput, calls=%fused_computation.11 | convolution fusion | flops 339886080 | bytes 3244032 | tf_op jit(solution)/shard_map/dot_general | solution.py:232
  147.5 1.6 %collective-permute-done.35 = bf16[80,1152]{1,0:T(8,128)(2,1)S(1)} collective-permute-done((bf16[80,1152]{1,0:T(8,128)(2,1)S(1)}, bf16[80,1152]{1,0:T(8,128)(2,1)S(1)}, u32[]{:S(2)}, u32[]{:S(2)}) %collective-permute-start.35) | collective-permute-done | bytes 184352 | tf_op jit(solution)/shard_map/ppermute | solution.py:32
  149.1 2.9 %collective-permute-done.34 = bf16[80,1152]{1,0:T(8,128)(2,1)S(1)} collective-permute-done((bf16[80,1152]{1,0:T(8,128)(2,1)S(1)}, bf16[80,1152]{1,0:T(8,128)(2,1)S(1)}, u32[]{:S(2)}, u32[]{:S(2)}) %collective-permute-start.34) | collective-permute-done | bytes 184352 | tf_op jit(solution)/shard_map/ppermute | solution.py:32
  152.1 3.6 %collective-permute-start.37 = (bf16[80,1152]{1,0:T(8,128)(2,1)S(1)}, bf16[80,1152]{1,0:T(8,128)(2,1)S(1)}, u32[]{:S(2)}, u32[]{:S(2)}) collective-permute-start(bf16[80,1152]{1,0:T(8,128)(2,1)S(1)} %add_convert_fusion.3), channel_id=1, source_target_pairs={{0,8},{1,9},{2,10},{3,11},{4,12},{5,13},{6,14},{7,15},{8,0},{9,1},... | collective-permute-start | bytes 552968 | tf_op jit(solution)/shard_map/ppermute | solution.py:32
  (166 shorter events, 32.6 us)
Async XLA Ops:
  4.3 18.2 %collective-permute-start.2 = (bf16[208,1152]{1,0:T(8,128)(2,1)S(1)}, bf16[208,1152]{1,0:T(8,128)(2,1)S(1)}, u32[]{:S(2)}, u32[]{:S(2)}) collective-permute-start(bf16[208,1152]{1,0:T(8,128)(2,1)S(1)} %get-tuple-element.24), channel_id=1, source_target_pairs={{0,1},{1,0},{2,3},{3,2},{4,5},{5,4},{6,7},{7,6},{8,9},{9,8},{10,11... | collective-permute-start | bytes 1437704 | tf_op jit(solution)/shard_map/ppermute | solution.py:32
  8.2 16.4 %collective-permute-start.1 = (bf16[208,1152]{1,0:T(8,128)(2,1)S(1)}, bf16[208,1152]{1,0:T(8,128)(2,1)S(1)}, u32[]{:S(2)}, u32[]{:S(2)}) collective-permute-start(bf16[208,1152]{1,0:T(8,128)(2,1)S(1)} %get-tuple-element.24), channel_id=1, source_target_pairs={{0,2},{1,3},{2,4},{3,5},{4,6},{5,7},{6,0},{7,1},{8,10},{9,11},{10,... | collective-permute-start | bytes 1437704 | tf_op jit(solution)/shard_map/ppermute | solution.py:32
  9.4 15.0 %collective-permute-start = (bf16[208,1152]{1,0:T(8,128)(2,1)S(1)}, bf16[208,1152]{1,0:T(8,128)(2,1)S(1)}, u32[]{:S(2)}, u32[]{:S(2)}) collective-permute-start(bf16[208,1152]{1,0:T(8,128)(2,1)S(1)} %get-tuple-element.24), channel_id=1, source_target_pairs={{0,6},{1,7},{2,0},{3,1},{4,2},{5,3},{6,4},{7,5},{8,14},{9,15},{10,... | collective-permute-start | bytes 1437704 | tf_op jit(solution)/shard_map/ppermute | solution.py:32
  10.8 8.5 %collective-permute-start.10 = (bf16[128,1152]{1,0:T(8,128)(2,1)S(1)}, bf16[128,1152]{1,0:T(8,128)(2,1)S(1)}, u32[]{:S(2)}, u32[]{:S(2)}) collective-permute-start(bf16[128,1152]{1,0:T(8,128)(2,1)S(1)} %get-tuple-element.26), channel_id=1, source_target_pairs={{0,96},{1,97},{2,98},{3,99},{4,100},{5,101},{6,102},{7,103},{8,104... | collective-permute-start | bytes 884744 | tf_op jit(solution)/shard_map/ppermute | solution.py:32
  14.6 7.9 %collective-permute-start.12 = (bf16[128,1152]{1,0:T(8,128)(2,1)S(1)}, bf16[128,1152]{1,0:T(8,128)(2,1)S(1)}, u32[]{:S(2)}, u32[]{:S(2)}) collective-permute-start(bf16[128,1152]{1,0:T(8,128)(2,1)S(1)} %get-tuple-element.26), channel_id=1, source_target_pairs={{0,32},{1,33},{2,34},{3,35},{4,36},{5,37},{6,38},{7,39},{8,40},{9,... | collective-permute-start | bytes 884744 | tf_op jit(solution)/shard_map/ppermute | solution.py:32
  22.9 11.8 %collective-permute-start.5 = (bf16[208,1152]{1,0:T(8,128)(2,1)S(1)}, bf16[208,1152]{1,0:T(8,128)(2,1)S(1)}, u32[]{:S(2)}, u32[]{:S(2)}) collective-permute-start(bf16[208,1152]{1,0:T(8,128)(2,1)S(1)} %collective-permute-done.2), channel_id=1, source_target_pairs={{0,6},{1,7},{2,0},{3,1},{4,2},{5,3},{6,4},{7,5},{8,14},{9,15},{10,... | collective-permute-start | bytes 1437704 | tf_op jit(solution)/shard_map/ppermute | solution.py:32
  24.2 10.4 %collective-permute-start.3 = (bf16[208,1152]{1,0:T(8,128)(2,1)S(1)}, bf16[208,1152]{1,0:T(8,128)(2,1)S(1)}, u32[]{:S(2)}, u32[]{:S(2)}) collective-permute-start(bf16[208,1152]{1,0:T(8,128)(2,1)S(1)} %collective-permute-done.2), channel_id=1, source_target_pairs={{0,2},{1,3},{2,4},{3,5},{4,6},{5,7},{6,0},{7,1},{8,10},{9,11},{10,... | collective-permute-start | bytes 1437704 | tf_op jit(solution)/shard_map/ppermute | solution.py:32
  28.1 14.4 %collective-permute-start.11 = (bf16[128,1152]{1,0:T(8,128)(2,1)S(1)}, bf16[128,1152]{1,0:T(8,128)(2,1)S(1)}, u32[]{:S(2)}, u32[]{:S(2)}) collective-permute-start(bf16[128,1152]{1,0:T(8,128)(2,1)S(1)} %collective-permute-done.9), channel_id=1, source_target_pairs={{0,96},{1,97},{2,98},{3,99},{4,100},{5,101},{6,102},{7,103},{8,104... | collective-permute-start | bytes 884744 | tf_op jit(solution)/shard_map/ppermute | solution.py:32
  28.9 15.6 %collective-permute-start.13 = (bf16[128,1152]{1,0:T(8,128)(2,1)S(1)}, bf16[128,1152]{1,0:T(8,128)(2,1)S(1)}, u32[]{:S(2)}, u32[]{:S(2)}) collective-permute-start(bf16[128,1152]{1,0:T(8,128)(2,1)S(1)} %collective-permute-done.9), channel_id=1, source_target_pairs={{0,32},{1,33},{2,34},{3,35},{4,36},{5,37},{6,38},{7,39},{8,40},{9,... | collective-permute-start | bytes 884744 | tf_op jit(solution)/shard_map/ppermute | solution.py:32
  34.7 19.7 %collective-permute-start.4 = (bf16[192,1152]{1,0:T(8,128)(2,1)S(1)}, bf16[192,1152]{1,0:T(8,128)(2,1)S(1)}, u32[]{:S(2)}, u32[]{:S(2)}) collective-permute-start(bf16[192,1152]{1,0:T(8,128)(2,1)S(1)} %pad_maximum_fusion.4), channel_id=1, source_target_pairs={{0,2},{1,3},{2,4},{3,5},{4,6},{5,7},{6,0},{7,1},{8,10},{9,11},{10,... | collective-permute-start | bytes 1327112 | tf_op jit(solution)/shard_map/ppermute | solution.py:32
  34.8 20.7 %collective-permute-start.6 = (bf16[224,1152]{1,0:T(8,128)(2,1)S(1)}, bf16[224,1152]{1,0:T(8,128)(2,1)S(1)}, u32[]{:S(2)}, u32[]{:S(2)}) collective-permute-start(bf16[224,1152]{1,0:T(8,128)(2,1)S(1)} %pad_maximum_fusion.3), channel_id=1, source_target_pairs={{0,6},{1,7},{2,0},{3,1},{4,2},{5,3},{6,4},{7,5},{8,14},{9,15},{10,... | collective-permute-start | bytes 1548296 | tf_op jit(solution)/shard_map/ppermute | solution.py:32
  37.6 20.1 %collective-permute-start.7 = (bf16[480,1152]{1,0:T(8,128)(2,1)S(1)}, bf16[480,1152]{1,0:T(8,128)(2,1)S(1)}, u32[]{:S(2)}, u32[]{:S(2)}) collective-permute-start(bf16[480,1152]{1,0:T(8,128)(2,1)S(1)} %slice_dynamic-update-slice_fusion.18.near), channel_id=1, source_target_pairs={{0,8},{1,9},{2,10},{3,11},{4,12},{5,13},{6,14},{7,15},{8,0},{9,1},... | collective-permute-start | bytes 3317768 | tf_op jit(solution)/shard_map/ppermute | solution.py:32
  42.6 8.7 %collective-permute-start.15 = (bf16[128,1152]{1,0:T(8,128)(2,1)S(1)}, bf16[128,1152]{1,0:T(8,128)(2,1)S(1)}, u32[]{:S(2)}, u32[]{:S(2)}) collective-permute-start(bf16[128,1152]{1,0:T(8,128)(2,1)S(1)} %pad_maximum_fusion.6), channel_id=1, source_target_pairs={{0,96},{1,97},{2,98},{3,99},{4,100},{5,101},{6,102},{7,103},{8,104... | collective-permute-start | bytes 884744 | tf_op jit(solution)/shard_map/ppermute | solution.py:32
  44.6 9.6 %collective-permute-start.14 = (bf16[128,1152]{1,0:T(8,128)(2,1)S(1)}, bf16[128,1152]{1,0:T(8,128)(2,1)S(1)}, u32[]{:S(2)}, u32[]{:S(2)}) collective-permute-start(bf16[128,1152]{1,0:T(8,128)(2,1)S(1)} %pad_maximum_fusion.5), channel_id=1, source_target_pairs={{0,32},{1,33},{2,34},{3,35},{4,36},{5,37},{6,38},{7,39},{8,40},{9,... | collective-permute-start | bytes 884744 | tf_op jit(solution)/shard_map/ppermute | solution.py:32
  81.6 14.7 %collective-permute-start.18 = (bf16[640,1152]{1,0:T(8,128)(2,1)S(1)}, bf16[640,1152]{1,0:T(8,128)(2,1)S(1)}, u32[]{:S(2)}, u32[]{:S(2)}) collective-permute-start(bf16[640,1152]{1,0:T(8,128)(2,1)S(1)} %get-tuple-element.30), channel_id=1, source_target_pairs={{0,8},{1,9},{2,10},{3,11},{4,12},{5,13},{6,14},{7,15},{8,0},{9,1},... | collective-permute-start | bytes 4423688 | tf_op jit(solution)/shard_map/ppermute | solution.py:32
  97.4 10.0 %collective-permute-start.22 = (bf16[1024,1152]{1,0:T(8,128)(2,1)}, bf16[1024,1152]{1,0:T(8,128)(2,1)}, u32[]{:S(2)}, u32[]{:S(2)}) collective-permute-start(bf16[1024,1152]{1,0:T(8,128)(2,1)} %fusion.9), channel_id=1, source_target_pairs={{0,8},{1,9},{2,10},{3,11},{4,12},{5,13},{6,14},{7,15},{8,0},{9,1},... | collective-permute-start | bytes 7077896 | tf_op jit(solution)/shard_map/ppermute | solution.py:32
  97.9 29.2 %collective-permute-start.29 = (bf16[512,1152]{1,0:T(8,128)(2,1)}, bf16[512,1152]{1,0:T(8,128)(2,1)S(1)}, u32[]{:S(2)}, u32[]{:S(2)}) collective-permute-start(bf16[512,1152]{1,0:T(8,128)(2,1)} %copy-done.9), channel_id=1, source_target_pairs={{0,1},{1,0},{2,3},{3,2},{4,5},{5,4},{6,7},{7,6},{8,9},{9,8},{10,11... | collective-permute-start | bytes 3538952 | tf_op jit(solution)/shard_map/ppermute | solution.py:32
  102.8 9.7 %collective-permute-start.21 = (bf16[160,1152]{1,0:T(8,128)(2,1)S(1)}, bf16[160,1152]{1,0:T(8,128)(2,1)S(1)}, u32[]{:S(2)}, u32[]{:S(2)}) collective-permute-start(bf16[160,1152]{1,0:T(8,128)(2,1)S(1)} %get-tuple-element.58), channel_id=1, source_target_pairs={{0,6},{1,7},{2,0},{3,1},{4,2},{5,3},{6,4},{7,5},{8,14},{9,15},{10,... | collective-permute-start | bytes 1105928 | tf_op jit(solution)/shard_map/ppermute | solution.py:32
  102.9 18.8 %collective-permute-start.20 = (bf16[160,1152]{1,0:T(8,128)(2,1)S(1)}, bf16[160,1152]{1,0:T(8,128)(2,1)S(1)}, u32[]{:S(2)}, u32[]{:S(2)}) collective-permute-start(bf16[160,1152]{1,0:T(8,128)(2,1)S(1)} %get-tuple-element.59), channel_id=1, source_target_pairs={{0,2},{1,3},{2,4},{3,5},{4,6},{5,7},{6,0},{7,1},{8,10},{9,11},{10,... | collective-permute-start | bytes 1105928 | tf_op jit(solution)/shard_map/ppermute | solution.py:32
  104.4 17.4 %collective-permute-start.19 = (bf16[160,1152]{1,0:T(8,128)(2,1)S(1)}, bf16[160,1152]{1,0:T(8,128)(2,1)S(1)}, u32[]{:S(2)}, u32[]{:S(2)}) collective-permute-start(bf16[160,1152]{1,0:T(8,128)(2,1)S(1)} %get-tuple-element.57), channel_id=1, source_target_pairs={{0,4},{1,5},{2,6},{3,7},{4,0},{5,1},{6,2},{7,3},{8,12},{9,13},{10,... | collective-permute-start | bytes 1105928 | tf_op jit(solution)/shard_map/ppermute | solution.py:32
  109.9 12.1 %collective-permute-start.24 = (bf16[128,1152]{1,0:T(8,128)(2,1)S(1)}, bf16[128,1152]{1,0:T(8,128)(2,1)S(1)}, u32[]{:S(2)}, u32[]{:S(2)}) collective-permute-start(bf16[128,1152]{1,0:T(8,128)(2,1)S(1)} %get-tuple-element.52), channel_id=1, source_target_pairs={{0,96},{1,97},{2,98},{3,99},{4,100},{5,101},{6,102},{7,103},{8,104... | collective-permute-start | bytes 884744 | tf_op jit(solution)/shard_map/ppermute | solution.py:32
  112.6 9.5 %collective-permute-start.23 = (bf16[128,1152]{1,0:T(8,128)(2,1)S(1)}, bf16[128,1152]{1,0:T(8,128)(2,1)S(1)}, u32[]{:S(2)}, u32[]{:S(2)}) collective-permute-start(bf16[128,1152]{1,0:T(8,128)(2,1)S(1)} %get-tuple-element.54), channel_id=1, source_target_pairs={{0,32},{1,33},{2,34},{3,35},{4,36},{5,37},{6,38},{7,39},{8,40},{9,... | collective-permute-start | bytes 884744 | tf_op jit(solution)/shard_map/ppermute | solution.py:32
  122.3 20.5 %collective-permute-start.26 = (bf16[256,1152]{1,0:T(8,128)(2,1)S(1)}, bf16[256,1152]{1,0:T(8,128)(2,1)S(1)}, u32[]{:S(2)}, u32[]{:S(2)}) collective-permute-start(bf16[256,1152]{1,0:T(8,128)(2,1)S(1)} %get-tuple-element.38), channel_id=1, source_target_pairs={{0,96},{1,97},{2,98},{3,99},{4,100},{5,101},{6,102},{7,103},{8,104... | collective-permute-start | bytes 1769480 | tf_op jit(solution)/shard_map/ppermute | solution.py:32
  122.4 20.4 %collective-permute-start.25 = (bf16[256,1152]{1,0:T(8,128)(2,1)S(1)}, bf16[256,1152]{1,0:T(8,128)(2,1)S(1)}, u32[]{:S(2)}, u32[]{:S(2)}) collective-permute-start(bf16[256,1152]{1,0:T(8,128)(2,1)S(1)} %get-tuple-element.37), channel_id=1, source_target_pairs={{0,32},{1,33},{2,34},{3,35},{4,36},{5,37},{6,38},{7,39},{8,40},{9,... | collective-permute-start | bytes 1769480 | tf_op jit(solution)/shard_map/ppermute | solution.py:32
  123.9 6.0 %collective-permute-start.27 = (bf16[80,1152]{1,0:T(8,128)(2,1)S(1)}, bf16[80,1152]{1,0:T(8,128)(2,1)S(1)}, u32[]{:S(2)}, u32[]{:S(2)}) collective-permute-start(bf16[80,1152]{1,0:T(8,128)(2,1)S(1)} %slice.373), channel_id=1, source_target_pairs={{0,1},{1,0},{2,3},{3,2},{4,5},{5,4},{6,7},{7,6},{8,9},{9,8},{10,11... | collective-permute-start | bytes 552968 | tf_op jit(solution)/shard_map/ppermute | solution.py:32
  127.4 7.6 %collective-permute-start.32 = (bf16[128,1152]{1,0:T(8,128)(2,1)S(1)}, bf16[128,1152]{1,0:T(8,128)(2,1)S(1)}, u32[]{:S(2)}, u32[]{:S(2)}) collective-permute-start(bf16[128,1152]{1,0:T(8,128)(2,1)S(1)} %get-tuple-element.61), channel_id=1, source_target_pairs={{0,6},{1,7},{2,0},{3,1},{4,2},{5,3},{6,4},{7,5},{8,14},{9,15},{10,... | collective-permute-start | bytes 884744 | tf_op jit(solution)/shard_map/ppermute | solution.py:32
  127.5 15.0 %collective-permute-start.31 = (bf16[128,1152]{1,0:T(8,128)(2,1)S(1)}, bf16[128,1152]{1,0:T(8,128)(2,1)S(1)}, u32[]{:S(2)}, u32[]{:S(2)}) collective-permute-start(bf16[128,1152]{1,0:T(8,128)(2,1)S(1)} %get-tuple-element.62), channel_id=1, source_target_pairs={{0,2},{1,3},{2,4},{3,5},{4,6},{5,7},{6,0},{7,1},{8,10},{9,11},{10,... | collective-permute-start | bytes 884744 | tf_op jit(solution)/shard_map/ppermute | solution.py:32
  129.8 12.7 %collective-permute-start.30 = (bf16[128,1152]{1,0:T(8,128)(2,1)S(1)}, bf16[128,1152]{1,0:T(8,128)(2,1)S(1)}, u32[]{:S(2)}, u32[]{:S(2)}) collective-permute-start(bf16[128,1152]{1,0:T(8,128)(2,1)S(1)} %get-tuple-element.60), channel_id=1, source_target_pairs={{0,4},{1,5},{2,6},{3,7},{4,0},{5,1},{6,2},{7,3},{8,12},{9,13},{10,... | collective-permute-start | bytes 884744 | tf_op jit(solution)/shard_map/ppermute | solution.py:32
  135.0 7.7 %collective-permute-start.28 = (bf16[80,1152]{1,0:T(8,128)(2,1)S(1)}, bf16[80,1152]{1,0:T(8,128)(2,1)S(1)}, u32[]{:S(2)}, u32[]{:S(2)}) collective-permute-start(bf16[80,1152]{1,0:T(8,128)(2,1)S(1)} %add_convert_fusion.5), channel_id=1, source_target_pairs={{0,16},{1,17},{2,18},{3,19},{4,20},{5,21},{6,22},{7,23},{8,24},{9,... | collective-permute-start | bytes 552968 | tf_op jit(solution)/shard_map/ppermute | solution.py:32
  143.2 6.0 %collective-permute-start.35 = (bf16[80,1152]{1,0:T(8,128)(2,1)S(1)}, bf16[80,1152]{1,0:T(8,128)(2,1)S(1)}, u32[]{:S(2)}, u32[]{:S(2)}) collective-permute-start(bf16[80,1152]{1,0:T(8,128)(2,1)S(1)} %add_convert_fusion.4), channel_id=1, source_target_pairs={{0,32},{1,33},{2,34},{3,35},{4,36},{5,37},{6,38},{7,39},{8,40},{9,... | collective-permute-start | bytes 552968 | tf_op jit(solution)/shard_map/ppermute | solution.py:32
  144.6 7.4 %collective-permute-start.34 = (bf16[80,1152]{1,0:T(8,128)(2,1)S(1)}, bf16[80,1152]{1,0:T(8,128)(2,1)S(1)}, u32[]{:S(2)}, u32[]{:S(2)}) collective-permute-start(bf16[80,1152]{1,0:T(8,128)(2,1)S(1)} %add_convert_fusion.4), channel_id=1, source_target_pairs={{0,64},{1,65},{2,66},{3,67},{4,68},{5,69},{6,70},{7,71},{8,72},{9,... | collective-permute-start | bytes 552968 | tf_op jit(solution)/shard_map/ppermute | solution.py:32
  144.6 11.1 %collective-permute-start.33 = (bf16[128,1152]{1,0:T(8,128)(2,1)S(1)}, bf16[128,1152]{1,0:T(8,128)(2,1)S(1)}, u32[]{:S(2)}, u32[]{:S(2)}) collective-permute-start(bf16[128,1152]{1,0:T(8,128)(2,1)S(1)} %slice.372), channel_id=1, source_target_pairs={{0,16},{1,17},{2,18},{3,19},{4,20},{5,21},{6,22},{7,23},{8,24},{9,... | collective-permute-start | bytes 884744 | tf_op jit(solution)/shard_map/ppermute | solution.py:32
  (24 other events, 166.8 us)
where the time goes:
time: 161 us; the launch traced here: 158 us
  waiting for transfers between devices  57.5 us (36%)
  starting transfers between devices  40.4 us (25%)
  matrix products  39.2 us (24%)
  other arithmetic  9.95 us (6%)
  local copies, waits for them, and re-layouts  6.01 us (4%)
  between operations  2.92 us (2%)
  Pallas kernels  2.21 us (1%)
    ppermute x38, waiting for transfers between devices, shift(): return lax.ppermute(value, AXES, pairs)  57.5 us
    ppermute x38, starting transfers between devices, shift(): return lax.ppermute(value, AXES, pairs)  40.4 us
    dot_general x4, matrix products, back_t(): lax.dot_general(pg, e, (((0,), (0,)), ((), ())), preferred_element_type=F32)  20.7 us
    dot_general x1, matrix products, pair(): lax.dot_general(e, t, (((1,), (1,)), ((), ())), preferred_element_type=F32)  6.91 us
    unnamed x58, local copies, waits for them, and re-layouts  5.23 us
    dot_general x1, matrix products, embed(): raw = jnp.dot(rows, weight, preferred_element_type=F32)  3.63 us
  transfers between devices with their start and end apart: 38, of which 16 were waited for; matrix products, arithmetic and copies ran while one was open for 20% of the time, Pallas kernels for 0%

commit v1 on v0

--- a/solution.py
+++ b/solution.py
@@ -116,24 +116,31 @@
     )(pos, *parts)
 
 
-def spread_kernel(pos, whole, keep, send):
+def give_kernel(pos, whole, send):
     c = pos[2]
     for dx in range(4):
         for dy in range(2):
-            k = dx * 2 + dy
-            base = block_row(pos, dx, dy)
-            keep[pl.ds(k * 80, 80), :] = whole[pl.ds(pl.multiple_of(base + c * 64, 16), 80), :]
-            send[pl.ds(k * 80, 80), :] = whole[pl.ds(pl.multiple_of(base + (1 - c) * 64, 16), 80), :]
-
-
-def spread(pos, whole):
+            row = pl.multiple_of(block_row(pos, dx, dy) + (1 - c) * 64, 16)
+            send[pl.ds((dx * 2 + dy) * 80, 80), :] = whole[pl.ds(row, 80), :]
+
+
+def take_kernel(pos, whole, got, out):
+    c = pos[2]
+    for dx in range(4):
+        for dy in range(2):
+            row = pl.multiple_of(block_row(pos, dx, dy) + c * 64, 16)
+            at = pl.ds((dx * 2 + dy) * 80, 80)
+            out[at, :] = (whole[pl.ds(row, 80), :].astype(F32) + got[at, :].astype(F32)).astype(BF)
+
+
+def by_blocks(kernel, pos, *arrays):
     return pl.pallas_call(
-        spread_kernel,
-        out_shape=[jax.ShapeDtypeStruct((640, 1152), BF)] * 2,
-        in_specs=[pl.BlockSpec(memory_space=pltpu.SMEM), pl.BlockSpec(memory_space=pltpu.VMEM)],
-        out_specs=[pl.BlockSpec(memory_space=pltpu.VMEM)] * 2,
+        kernel,
+        out_shape=jax.ShapeDtypeStruct((640, 1152), BF),
+        in_specs=[pl.BlockSpec(memory_space=pltpu.SMEM)] + [pl.BlockSpec(memory_space=pltpu.VMEM)] * len(arrays),
+        out_specs=pl.BlockSpec(memory_space=pltpu.VMEM),
         compiler_params=pltpu.CompilerParams(vmem_limit_bytes=32 * 2**20),
-    )(pos, whole)
+    )(pos, *arrays)
 
 
 def local(pooled, text_feats, out_weight, logit_scale, logit_bias):
@@ -165,7 +172,7 @@
     fb = shift(jnp.concatenate([t_p[64:], u_p[64:]], 0), "z", -1)
     t_near = jnp.concatenate([text_emb, text_oth, t_p, u_p, t_m, u_m], 0)
     t_far = jnp.concatenate([fa[:64], fb[:64], fa[64:], fb[64:]], 0)
-    t_near, t_far, _ = join(t_near, t_far, w_far_c)
+    t_far, _ = join(t_far, w_far_c)
     c_near = shift(t_near, "c", 1)
     c_far = shift(t_far, "c", 1)
     texts = jnp.concatenate([t_near[:512], t_far, t_near[512:], c_near[:512], c_far, c_near[512:]], 0)
@@ -200,13 +207,12 @@
 
     r1_here = shift(r1, "yh", 1)
     gw = (back_t(images[:512], r0) + back_t(images[512:], r1)).astype(BF)
-    keep, send = spread(pos, gw)
-    send = shift(send, "c", 1)
+    send = shift(by_blocks(give_kernel, pos, gw), "c", 1)
     gt_send = back_t(grads[:, 1024:], emb)
-    keep, send, gt_send = join(keep, send, gt_send)
+    send, gt_send = join(send, gt_send)
     gt_send = gt_send.astype(BF)
 
-    s, grads = join((keep.astype(F32) + send.astype(F32)).astype(BF), grads)
+    s, grads = join(by_blocks(take_kernel, pos, gw, send), grads)
     s = near_sum(s, "x", 160)
     gt = back_t(grads[:, :1024], emb)
     gt = gt + shift(gt_send, "c", 1).astype(F32)

time: 161 us -> 161 us (level)
  other arithmetic: 9.95 us -> 7.73 us
  local copies, waits for them, and re-layouts: 6.01 us -> 7.74 us
    convert_element_type x1 -> x0, other arithmetic: 2.17 us -> none  [local(): s, grads = join((keep.astype(F32) + send.astype(F32)).astype(BF), grads)]
    unnamed x58 -> x60, local copies, waits for them, and re-layouts: 5.23 us -> 6.93 us
  transfers between devices with their start and end apart: 38 -> 38, of which waited for: 16 -> 16; matrix products, arithmetic and copies ran while one was open for 20% -> 19% of each run, Pallas kernels for 0% -> 1%
where the time goes in v1:
time: 161 us; the launch traced here: 158 us
  waiting for transfers between devices  57 us (35%)
  starting transfers between devices  40.5 us (25%)
  matrix products  39.1 us (24%)
  local copies, waits for them, and re-layouts  7.74 us (5%)
  other arithmetic  7.73 us (5%)
  Pallas kernels  3.04 us (2%)
  between operations  2.88 us (2%)
    ppermute x38, waiting for transfers between devices, shift(): return lax.ppermute(value, AXES, pairs)  57 us
    ppermute x38, starting transfers between devices, shift(): return lax.ppermute(value, AXES, pairs)  40.5 us
    dot_general x4, matrix products, back_t(): lax.dot_general(pg, e, (((0,), (0,)), ((), ())), preferred_element_type=F32)  20.7 us
    unnamed x60, local copies, waits for them, and re-layouts  6.93 us
    dot_general x1, matrix products, pair(): lax.dot_general(e, t, (((1,), (1,)), ((), ())), preferred_element_type=F32)  6.91 us
    dot_general x1, matrix products, embed(): raw = jnp.dot(rows, weight, preferred_element_type=F32)  3.62 us
  transfers between devices with their start and end apart: 38, of which 16 were waited for; matrix products, arithmetic and copies ran while one was open for 19% of the time, Pallas kernels for 1%

profile of v1, /device:TPU:1, one launch (start us, length us, event | category | flops | bytes accessed | tf_op | source)
XLA Modules:
  0.0 158.0 jit_solution(2617646908141264265)
XLA Ops:
  4.3 3.8 %collective-permute-start.2 = (bf16[208,1152]{1,0:T(8,128)(2,1)S(1)}, bf16[208,1152]{1,0:T(8,128)(2,1)S(1)}, u32[]{:S(2)}, u32[]{:S(2)}) collective-permute-start(bf16[208,1152]{1,0:T(8,128)(2,1)S(1)} %get-tuple-element.20), channel_id=1, source_target_pairs={{0,1},{1,0},{2,3},{3,2},{4,5},{5,4},{6,7},{7,6},{8,9},{9,8},{10,11... | collective-permute-start | bytes 1437704 | tf_op jit(solution)/shard_map/ppermute | solution.py:32
  9.4 1.5 collective-permute-start
  10.8 3.8 %collective-permute-start.10 = (bf16[128,1152]{1,0:T(8,128)(2,1)S(1)}, bf16[128,1152]{1,0:T(8,128)(2,1)S(1)}, u32[]{:S(2)}, u32[]{:S(2)}) collective-permute-start(bf16[128,1152]{1,0:T(8,128)(2,1)S(1)} %get-tuple-element.22), channel_id=1, source_target_pairs={{0,96},{1,97},{2,98},{3,99},{4,100},{5,101},{6,102},{7,103},{8,104... | collective-permute-start | bytes 884744 | tf_op jit(solution)/shard_map/ppermute | solution.py:32
  16.0 3.4 %collective-permute-done.10 = bf16[128,1152]{1,0:T(8,128)(2,1)S(1)} collective-permute-done((bf16[128,1152]{1,0:T(8,128)(2,1)S(1)}, bf16[128,1152]{1,0:T(8,128)(2,1)S(1)}, u32[]{:S(2)}, u32[]{:S(2)}) %collective-permute-start.10) | collective-permute-done | bytes 294944 | tf_op jit(solution)/shard_map/ppermute | solution.py:32
  19.4 3.1 %collective-permute-done.12 = bf16[128,1152]{1,0:T(8,128)(2,1)S(1)} collective-permute-done((bf16[128,1152]{1,0:T(8,128)(2,1)S(1)}, bf16[128,1152]{1,0:T(8,128)(2,1)S(1)}, u32[]{:S(2)}, u32[]{:S(2)}) %collective-permute-start.12) | collective-permute-done | bytes 294944 | tf_op jit(solution)/shard_map/ppermute | solution.py:32
  24.6 3.5 %collective-permute-done.9 = bf16[128,1152]{1,0:T(8,128)(2,1)S(1)} collective-permute-done((bf16[128,1152]{1,0:T(8,128)(2,1)S(1)}, bf16[128,1152]{1,0:T(8,128)(2,1)S(1)}, u32[]{:S(2)}, u32[]{:S(2)}) %collective-permute-start.9) | collective-permute-done | bytes 294944 | tf_op jit(solution)/shard_map/ppermute | solution.py:32
  29.7 4.9 %collective-permute-done.3 = bf16[208,1152]{1,0:T(8,128)(2,1)S(1)} collective-permute-done((bf16[208,1152]{1,0:T(8,128)(2,1)S(1)}, bf16[208,1152]{1,0:T(8,128)(2,1)S(1)}, u32[]{:S(2)}, u32[]{:S(2)}) %collective-permute-start.3) | collective-permute-done | bytes 479264 | tf_op jit(solution)/shard_map/ppermute | solution.py:32
  34.8 2.7 %collective-permute-start.6 = (bf16[224,1152]{1,0:T(8,128)(2,1)S(1)}, bf16[224,1152]{1,0:T(8,128)(2,1)S(1)}, u32[]{:S(2)}, u32[]{:S(2)}) collective-permute-start(bf16[224,1152]{1,0:T(8,128)(2,1)S(1)} %pad_maximum_fusion.3), channel_id=1, source_target_pairs={{0,6},{1,7},{2,0},{3,1},{4,2},{5,3},{6,4},{7,5},{8,14},{9,15},{10,... | collective-permute-start | bytes 1548296 | tf_op jit(solution)/shard_map/ppermute | solution.py:32
  37.6 4.8 %collective-permute-start.7 = (bf16[480,1152]{1,0:T(8,128)(2,1)S(1)}, bf16[480,1152]{1,0:T(8,128)(2,1)S(1)}, u32[]{:S(2)}, u32[]{:S(2)}) collective-permute-start(bf16[480,1152]{1,0:T(8,128)(2,1)S(1)} %slice_dynamic-update-slice_fusion.16.near), channel_id=1, source_target_pairs={{0,8},{1,9},{2,10},{3,11},{4,12},{5,13},{6,14},{7,15},{8,0},{9,1},... | collective-permute-start | bytes 3317768 | tf_op jit(solution)/shard_map/ppermute | solution.py:32
  42.6 2.0 %collective-permute-start.15 = (bf16[128,1152]{1,0:T(8,128)(2,1)S(1)}, bf16[128,1152]{1,0:T(8,128)(2,1)S(1)}, u32[]{:S(2)}, u32[]{:S(2)}) collective-permute-start(bf16[128,1152]{1,0:T(8,128)(2,1)S(1)} %pad_maximum_fusion.6), channel_id=1, source_target_pairs={{0,96},{1,97},{2,98},{3,99},{4,100},{5,101},{6,102},{7,103},{8,104... | collective-permute-start | bytes 884744 | tf_op jit(solution)/shard_map/ppermute | solution.py:32
  44.8 6.5 %collective-permute-done.15 = bf16[128,1152]{1,0:T(8,128)(2,1)S(1)} collective-permute-done((bf16[128,1152]{1,0:T(8,128)(2,1)S(1)}, bf16[128,1152]{1,0:T(8,128)(2,1)S(1)}, u32[]{:S(2)}, u32[]{:S(2)}) %collective-permute-start.15) | collective-permute-done | bytes 294944 | tf_op jit(solution)/shard_map/ppermute | solution.py:32
  51.3 2.9 %collective-permute-done.14 = bf16[128,1152]{1,0:T(8,128)(2,1)S(1)} collective-permute-done((bf16[128,1152]{1,0:T(8,128)(2,1)S(1)}, bf16[128,1152]{1,0:T(8,128)(2,1)S(1)}, u32[]{:S(2)}, u32[]{:S(2)}) %collective-permute-start.14) | collective-permute-done | bytes 294944 | tf_op jit(solution)/shard_map/ppermute | solution.py:32
  58.5 3.6 %multiply_reduce_fusion = (f32[1024]{0:T(1024)S(1)}, f32[1024,1152]{1,0:T(8,128)S(1)}) fusion(bf16[1024,1152]{1,0:T(8,128)(2,1)S(1)} %get-tuple-element.59, bf16[1152,1152]{1,0:T(8,128)(2,1)S(1)} %shard_map.77), kind=kOutput, calls=%fused_computation.5 | convolution fusion | flops 2720267264 | bytes 9736192 | tf_op jit(solution)/shard_map/dot_general | solution.py:181
  63.0 6.9 %multiply_convert_fusion = bf16[1024,2048]{1,0:T(8,128)(2,1)S(1)} fusion(bf16[1024,1152]{1,0:T(8,128)(2,1)S(1)} %divide_convert_fusion, bf16[2048,1152]{1,0:T(8,128)(2,1)S(1)} %slice_dynamic-update-slice_fusion.1, f32[]{:T(128)} %bitcast.22, f32[]{:T(128)} %bitcast.20), kind=kOutput, calls=%fused_computation.1 | convolution fusion | flops 4846518272 | bytes 11272200 | tf_op jit(solution)/shard_map/dot_general | solution.py:188
  70.3 2.9 %fusion.13 = f32[512,1152]{1,0:T(8,128)S(1)} fusion(bf16[2048,1152]{1,0:T(8,128)(2,1)S(1)} %slice_dynamic-update-slice_fusion.1, bf16[1024,2048]{1,0:T(8,128)(2,1)S(1)} %fusion.26), kind=kOutput, calls=%fused_computation.24 | convolution fusion | flops 2415919104 | bytes 9175040 | tf_op jit(solution)/shard_map/dot_general | solution.py:205
  73.1 3.1 %fusion.5 = (f32[512]{0:T(512)S(1)}, f32[512]{0:T(512)S(1)}, f32[512,1152]{1,0:T(8,128)S(1)}) fusion(bf16[1024,1152]{1,0:T(8,128)(2,1)S(1)} %divide_convert_fusion, f32[512,1152]{1,0:T(8,128)S(1)} %fusion.13, bf16[2048,1152]{1,0:T(8,128)(2,1)S(1)} %slice_dynamic-update-slice_fusion.1, bf16[1024,2048]{1,0:T(8,128)(2,1)S(1)} %fusion.26), kind=kOutput, calls=%fused_computation.15 | convolution fusion | flops 2419457024 | bytes 13897728 | tf_op jit(solution)/shard_map/dot_general | solution.py:206
  77.2 1.7 %fusion.38 = f32[1152,1152]{1,0:T(8,128)S(1)} fusion(bf16[512,1152]{1,0:T(8,128)(2,1)S(1)} %get-tuple-element.61, bf16[512,1152]{1,0:T(8,128)(2,1)S(1)} %get-tuple-element.32), kind=kOutput, calls=%fused_computation.121 | convolution fusion | flops 1358954496 | bytes 7667712 | tf_op jit(solution)/shard_map/dot_general | solution.py:199
  79.0 1.8 %fusion.whole = bf16[1152,1152]{1,0:T(8,128)(2,1)S(1)} fusion(f32[1152,1152]{1,0:T(8,128)S(1)} %fusion.38, bf16[512,1152]{1,0:T(8,128)(2,1)S(1)} %get-tuple-element.58, bf16[512,1152]{1,0:T(8,128)(2,1)S(1)} %get-tuple-element.47), kind=kOutput, calls=%fused_computation.2 | convolution fusion | flops 1361608704 | bytes 10321920 | tf_op jit(solution)/shard_map/dot_general | solution.py:199
  82.0 14.1 %fusion.9 = bf16[1024,1152]{1,0:T(8,128)(2,1)} fusion(bf16[1024,1152]{1,0:T(8,128)(2,1)S(1)} %divide_convert_fusion, bf16[1024,2048]{1,0:T(8,128)(2,1)S(1)} %fusion.26), kind=kOutput, calls=%fused_computation.20 | convolution fusion | flops 2415919104 | bytes 6815744 | tf_op jit(solution)/shard_map/dot_general | solution.py:199
  97.7 2.7 %collective-permute-start.29 = (bf16[512,1152]{1,0:T(8,128)(2,1)}, bf16[512,1152]{1,0:T(8,128)(2,1)S(1)}, u32[]{:S(2)}, u32[]{:S(2)}) collective-permute-start(bf16[512,1152]{1,0:T(8,128)(2,1)} %copy-done.12), channel_id=1, source_target_pairs={{0,1},{1,0},{2,3},{3,2},{4,5},{5,4},{6,7},{7,6},{8,9},{9,8},{10,11... | collective-permute-start | bytes 3538952 | tf_op jit(solution)/shard_map/ppermute | solution.py:32
  104.6 3.0 %fusion.15 = f32[1024,1152]{1,0:T(8,128)S(1)} fusion(bf16[1024,1152]{1,0:T(8,128)(2,1)S(1)} %copy-done.11, bf16[1024,2048]{1,0:T(8,128)(2,1)S(1)} %copy-done.17), kind=kOutput, calls=%fused_computation.26 | convolution fusion | flops 2415919104 | bytes 9175040 | tf_op jit(solution)/shard_map/dot_general | solution.py:199
  107.7 2.4 %fusion.31 = (bf16[1024,1152]{1,0:T(8,128)(2,1)S(1)}, f32[1024,1152]{1,0:T(8,128)S(1)}) fusion(f32[1024,1152]{1,0:T(8,128)S(1)} %fusion.15, bf16[1024,1152]{1,0:T(8,128)(2,1)} %collective-permute-done.22), kind=kLoop, calls=%fused_computation.114 | loop fusion | flops 3538944 | bytes 14155776 | tf_op jit(solution)/shard_map/convert.8
  110.3 2.3 %collective-permute-done.21 = bf16[160,1152]{1,0:T(8,128)(2,1)S(1)} collective-permute-done((bf16[160,1152]{1,0:T(8,128)(2,1)S(1)}, bf16[160,1152]{1,0:T(8,128)(2,1)S(1)}, u32[]{:S(2)}, u32[]{:S(2)}) %collective-permute-start.21) | collective-permute-done | bytes 368672 | tf_op jit(solution)/shard_map/ppermute | solution.py:32
  112.5 9.2 %collective-permute-done.20 = bf16[160,1152]{1,0:T(8,128)(2,1)S(1)} collective-permute-done((bf16[160,1152]{1,0:T(8,128)(2,1)S(1)}, bf16[160,1152]{1,0:T(8,128)(2,1)S(1)}, u32[]{:S(2)}, u32[]{:S(2)}) %collective-permute-start.20) | collective-permute-done | bytes 368672 | tf_op jit(solution)/shard_map/ppermute | solution.py:32
  122.3 1.5 collective-permute-start.25
  124.2 2.6 %collective-permute-done.29 = bf16[512,1152]{1,0:T(8,128)(2,1)S(1)} collective-permute-done((bf16[512,1152]{1,0:T(8,128)(2,1)}, bf16[512,1152]{1,0:T(8,128)(2,1)S(1)}, u32[]{:S(2)}, u32[]{:S(2)}) %collective-permute-start.29) | collective-permute-done | bytes 1179680 | tf_op jit(solution)/shard_map/ppermute | solution.py:32
  131.2 3.6 %collective-permute-done.32 = bf16[128,1152]{1,0:T(8,128)(2,1)S(1)} collective-permute-done((bf16[128,1152]{1,0:T(8,128)(2,1)S(1)}, bf16[128,1152]{1,0:T(8,128)(2,1)S(1)}, u32[]{:S(2)}, u32[]{:S(2)}) %collective-permute-start.32) | collective-permute-done | bytes 294944 | tf_op jit(solution)/shard_map/ppermute | solution.py:32
  134.9 7.4 %collective-permute-done.31 = bf16[128,1152]{1,0:T(8,128)(2,1)S(1)} collective-permute-done((bf16[128,1152]{1,0:T(8,128)(2,1)S(1)}, bf16[128,1152]{1,0:T(8,128)(2,1)S(1)}, u32[]{:S(2)}, u32[]{:S(2)}) %collective-permute-start.31) | collective-permute-done | bytes 294944 | tf_op jit(solution)/shard_map/ppermute | solution.py:32
  144.6 1.6 %convolution_convert_fusion = bf16[128,1152]{1,0:T(8,128)(2,1)} fusion(bf16[128,1152]{1,0:T(8,128)(2,1)S(1)} %add_convert_fusion.1, bf16[1152,1152]{1,0:T(8,128)(2,1)S(1)} %copy-done.1), kind=kOutput, calls=%fused_computation.10 | convolution fusion | flops 339886080 | bytes 3244032 | tf_op jit(solution)/shard_map/dot_general | solution.py:238
  147.3 1.6 %collective-permute-done.35 = bf16[80,1152]{1,0:T(8,128)(2,1)S(1)} collective-permute-done((bf16[80,1152]{1,0:T(8,128)(2,1)S(1)}, bf16[80,1152]{1,0:T(8,128)(2,1)S(1)}, u32[]{:S(2)}, u32[]{:S(2)}) %collective-permute-start.35) | collective-permute-done | bytes 184352 | tf_op jit(solution)/shard_map/ppermute | solution.py:32
  148.9 2.9 %collective-permute-done.34 = bf16[80,1152]{1,0:T(8,128)(2,1)S(1)} collective-permute-done((bf16[80,1152]{1,0:T(8,128)(2,1)S(1)}, bf16[80,1152]{1,0:T(8,128)(2,1)S(1)}, u32[]{:S(2)}, u32[]{:S(2)}) %collective-permute-start.34) | collective-permute-done | bytes 184352 | tf_op jit(solution)/shard_map/ppermute | solution.py:32
  151.9 3.6 %collective-permute-start.37 = (bf16[80,1152]{1,0:T(8,128)(2,1)S(1)}, bf16[80,1152]{1,0:T(8,128)(2,1)S(1)}, u32[]{:S(2)}, u32[]{:S(2)}) collective-permute-start(bf16[80,1152]{1,0:T(8,128)(2,1)S(1)} %add_convert_fusion.2), channel_id=1, source_target_pairs={{0,8},{1,9},{2,10},{3,11},{4,12},{5,13},{6,14},{7,15},{8,0},{9,1},... | collective-permute-start | bytes 552968 | tf_op jit(solution)/shard_map/ppermute | solution.py:32
  (168 shorter events, 33.7 us)
Async XLA Ops:
  4.3 18.2 %collective-permute-start.2 = (bf16[208,1152]{1,0:T(8,128)(2,1)S(1)}, bf16[208,1152]{1,0:T(8,128)(2,1)S(1)}, u32[]{:S(2)}, u32[]{:S(2)}) collective-permute-start(bf16[208,1152]{1,0:T(8,128)(2,1)S(1)} %get-tuple-element.20), channel_id=1, source_target_pairs={{0,1},{1,0},{2,3},{3,2},{4,5},{5,4},{6,7},{7,6},{8,9},{9,8},{10,11... | collective-permute-start | bytes 1437704 | tf_op jit(solution)/shard_map/ppermute | solution.py:32
  8.2 16.2 %collective-permute-start.1 = (bf16[208,1152]{1,0:T(8,128)(2,1)S(1)}, bf16[208,1152]{1,0:T(8,128)(2,1)S(1)}, u32[]{:S(2)}, u32[]{:S(2)}) collective-permute-start(bf16[208,1152]{1,0:T(8,128)(2,1)S(1)} %get-tuple-element.20), channel_id=1, source_target_pairs={{0,2},{1,3},{2,4},{3,5},{4,6},{5,7},{6,0},{7,1},{8,10},{9,11},{10,... | collective-permute-start | bytes 1437704 | tf_op jit(solution)/shard_map/ppermute | solution.py:32
  9.4 15.1 %collective-permute-start = (bf16[208,1152]{1,0:T(8,128)(2,1)S(1)}, bf16[208,1152]{1,0:T(8,128)(2,1)S(1)}, u32[]{:S(2)}, u32[]{:S(2)}) collective-permute-start(bf16[208,1152]{1,0:T(8,128)(2,1)S(1)} %get-tuple-element.20), channel_id=1, source_target_pairs={{0,6},{1,7},{2,0},{3,1},{4,2},{5,3},{6,4},{7,5},{8,14},{9,15},{10,... | collective-permute-start | bytes 1437704 | tf_op jit(solution)/shard_map/ppermute | solution.py:32
  10.8 8.5 %collective-permute-start.10 = (bf16[128,1152]{1,0:T(8,128)(2,1)S(1)}, bf16[128,1152]{1,0:T(8,128)(2,1)S(1)}, u32[]{:S(2)}, u32[]{:S(2)}) collective-permute-start(bf16[128,1152]{1,0:T(8,128)(2,1)S(1)} %get-tuple-element.22), channel_id=1, source_target_pairs={{0,96},{1,97},{2,98},{3,99},{4,100},{5,101},{6,102},{7,103},{8,104... | collective-permute-start | bytes 884744 | tf_op jit(solution)/shard_map/ppermute | solution.py:32
  14.6 7.9 %collective-permute-start.12 = (bf16[128,1152]{1,0:T(8,128)(2,1)S(1)}, bf16[128,1152]{1,0:T(8,128)(2,1)S(1)}, u32[]{:S(2)}, u32[]{:S(2)}) collective-permute-start(bf16[128,1152]{1,0:T(8,128)(2,1)S(1)} %get-tuple-element.22), channel_id=1, source_target_pairs={{0,32},{1,33},{2,34},{3,35},{4,36},{5,37},{6,38},{7,39},{8,40},{9,... | collective-permute-start | bytes 884744 | tf_op jit(solution)/shard_map/ppermute | solution.py:32
  22.9 11.8 %collective-permute-start.5 = (bf16[208,1152]{1,0:T(8,128)(2,1)S(1)}, bf16[208,1152]{1,0:T(8,128)(2,1)S(1)}, u32[]{:S(2)}, u32[]{:S(2)}) collective-permute-start(bf16[208,1152]{1,0:T(8,128)(2,1)S(1)} %collective-permute-done.2), channel_id=1, source_target_pairs={{0,6},{1,7},{2,0},{3,1},{4,2},{5,3},{6,4},{7,5},{8,14},{9,15},{10,... | collective-permute-start | bytes 1437704 | tf_op jit(solution)/shard_map/ppermute | solution.py:32
  24.2 10.4 %collective-permute-start.3 = (bf16[208,1152]{1,0:T(8,128)(2,1)S(1)}, bf16[208,1152]{1,0:T(8,128)(2,1)S(1)}, u32[]{:S(2)}, u32[]{:S(2)}) collective-permute-start(bf16[208,1152]{1,0:T(8,128)(2,1)S(1)} %collective-permute-done.2), channel_id=1, source_target_pairs={{0,2},{1,3},{2,4},{3,5},{4,6},{5,7},{6,0},{7,1},{8,10},{9,11},{10,... | collective-permute-start | bytes 1437704 | tf_op jit(solution)/shard_map/ppermute | solution.py:32
  28.1 14.4 %collective-permute-start.11 = (bf16[128,1152]{1,0:T(8,128)(2,1)S(1)}, bf16[128,1152]{1,0:T(8,128)(2,1)S(1)}, u32[]{:S(2)}, u32[]{:S(2)}) collective-permute-start(bf16[128,1152]{1,0:T(8,128)(2,1)S(1)} %collective-permute-done.9), channel_id=1, source_target_pairs={{0,96},{1,97},{2,98},{3,99},{4,100},{5,101},{6,102},{7,103},{8,104... | collective-permute-start | bytes 884744 | tf_op jit(solution)/shard_map/ppermute | solution.py:32
  28.9 15.6 %collective-permute-start.13 = (bf16[128,1152]{1,0:T(8,128)(2,1)S(1)}, bf16[128,1152]{1,0:T(8,128)(2,1)S(1)}, u32[]{:S(2)}, u32[]{:S(2)}) collective-permute-start(bf16[128,1152]{1,0:T(8,128)(2,1)S(1)} %collective-permute-done.9), channel_id=1, source_target_pairs={{0,32},{1,33},{2,34},{3,35},{4,36},{5,37},{6,38},{7,39},{8,40},{9,... | collective-permute-start | bytes 884744 | tf_op jit(solution)/shard_map/ppermute | solution.py:32
  34.6 19.6 %collective-permute-start.4 = (bf16[192,1152]{1,0:T(8,128)(2,1)S(1)}, bf16[192,1152]{1,0:T(8,128)(2,1)S(1)}, u32[]{:S(2)}, u32[]{:S(2)}) collective-permute-start(bf16[192,1152]{1,0:T(8,128)(2,1)S(1)} %pad_maximum_fusion.4), channel_id=1, source_target_pairs={{0,2},{1,3},{2,4},{3,5},{4,6},{5,7},{6,0},{7,1},{8,10},{9,11},{10,... | collective-permute-start | bytes 1327112 | tf_op jit(solution)/shard_map/ppermute | solution.py:32
  34.8 20.7 %collective-permute-start.6 = (bf16[224,1152]{1,0:T(8,128)(2,1)S(1)}, bf16[224,1152]{1,0:T(8,128)(2,1)S(1)}, u32[]{:S(2)}, u32[]{:S(2)}) collective-permute-start(bf16[224,1152]{1,0:T(8,128)(2,1)S(1)} %pad_maximum_fusion.3), channel_id=1, source_target_pairs={{0,6},{1,7},{2,0},{3,1},{4,2},{5,3},{6,4},{7,5},{8,14},{9,15},{10,... | collective-permute-start | bytes 1548296 | tf_op jit(solution)/shard_map/ppermute | solution.py:32
  37.6 20.1 %collective-permute-start.7 = (bf16[480,1152]{1,0:T(8,128)(2,1)S(1)}, bf16[480,1152]{1,0:T(8,128)(2,1)S(1)}, u32[]{:S(2)}, u32[]{:S(2)}) collective-permute-start(bf16[480,1152]{1,0:T(8,128)(2,1)S(1)} %slice_dynamic-update-slice_fusion.16.near), channel_id=1, source_target_pairs={{0,8},{1,9},{2,10},{3,11},{4,12},{5,13},{6,14},{7,15},{8,0},{9,1},... | collective-permute-start | bytes 3317768 | tf_op jit(solution)/shard_map/ppermute | solution.py:32
  42.6 8.7 %collective-permute-start.15 = (bf16[128,1152]{1,0:T(8,128)(2,1)S(1)}, bf16[128,1152]{1,0:T(8,128)(2,1)S(1)}, u32[]{:S(2)}, u32[]{:S(2)}) collective-permute-start(bf16[128,1152]{1,0:T(8,128)(2,1)S(1)} %pad_maximum_fusion.6), channel_id=1, source_target_pairs={{0,96},{1,97},{2,98},{3,99},{4,100},{5,101},{6,102},{7,103},{8,104... | collective-permute-start | bytes 884744 | tf_op jit(solution)/shard_map/ppermute | solution.py:32
  44.6 9.6 %collective-permute-start.14 = (bf16[128,1152]{1,0:T(8,128)(2,1)S(1)}, bf16[128,1152]{1,0:T(8,128)(2,1)S(1)}, u32[]{:S(2)}, u32[]{:S(2)}) collective-permute-start(bf16[128,1152]{1,0:T(8,128)(2,1)S(1)} %pad_maximum_fusion.5), channel_id=1, source_target_pairs={{0,32},{1,33},{2,34},{3,35},{4,36},{5,37},{6,38},{7,39},{8,40},{9,... | collective-permute-start | bytes 884744 | tf_op jit(solution)/shard_map/ppermute | solution.py:32
  81.5 14.6 %collective-permute-start.18 = (bf16[640,1152]{1,0:T(8,128)(2,1)S(1)}, bf16[640,1152]{1,0:T(8,128)(2,1)S(1)}, u32[]{:S(2)}, u32[]{:S(2)}) collective-permute-start(bf16[640,1152]{1,0:T(8,128)(2,1)S(1)} %shard_map.78), channel_id=1, source_target_pairs={{0,8},{1,9},{2,10},{3,11},{4,12},{5,13},{6,14},{7,15},{8,0},{9,1},... | collective-permute-start | bytes 4423688 | tf_op jit(solution)/shard_map/ppermute | solution.py:32
  97.2 10.4 %collective-permute-start.22 = (bf16[1024,1152]{1,0:T(8,128)(2,1)}, bf16[1024,1152]{1,0:T(8,128)(2,1)}, u32[]{:S(2)}, u32[]{:S(2)}) collective-permute-start(bf16[1024,1152]{1,0:T(8,128)(2,1)} %fusion.9), channel_id=1, source_target_pairs={{0,8},{1,9},{2,10},{3,11},{4,12},{5,13},{6,14},{7,15},{8,0},{9,1},... | collective-permute-start | bytes 7077896 | tf_op jit(solution)/shard_map/ppermute | solution.py:32
  97.7 29.2 %collective-permute-start.29 = (bf16[512,1152]{1,0:T(8,128)(2,1)}, bf16[512,1152]{1,0:T(8,128)(2,1)S(1)}, u32[]{:S(2)}, u32[]{:S(2)}) collective-permute-start(bf16[512,1152]{1,0:T(8,128)(2,1)} %copy-done.12), channel_id=1, source_target_pairs={{0,1},{1,0},{2,3},{3,2},{4,5},{5,4},{6,7},{7,6},{8,9},{9,8},{10,11... | collective-permute-start | bytes 3538952 | tf_op jit(solution)/shard_map/ppermute | solution.py:32
  102.8 9.7 %collective-permute-start.21 = (bf16[160,1152]{1,0:T(8,128)(2,1)S(1)}, bf16[160,1152]{1,0:T(8,128)(2,1)S(1)}, u32[]{:S(2)}, u32[]{:S(2)}) collective-permute-start(bf16[160,1152]{1,0:T(8,128)(2,1)S(1)} %get-tuple-element.50), channel_id=1, source_target_pairs={{0,6},{1,7},{2,0},{3,1},{4,2},{5,3},{6,4},{7,5},{8,14},{9,15},{10,... | collective-permute-start | bytes 1105928 | tf_op jit(solution)/shard_map/ppermute | solution.py:32
  102.9 18.9 %collective-permute-start.20 = (bf16[160,1152]{1,0:T(8,128)(2,1)S(1)}, bf16[160,1152]{1,0:T(8,128)(2,1)S(1)}, u32[]{:S(2)}, u32[]{:S(2)}) collective-permute-start(bf16[160,1152]{1,0:T(8,128)(2,1)S(1)} %get-tuple-element.51), channel_id=1, source_target_pairs={{0,2},{1,3},{2,4},{3,5},{4,6},{5,7},{6,0},{7,1},{8,10},{9,11},{10,... | collective-permute-start | bytes 1105928 | tf_op jit(solution)/shard_map/ppermute | solution.py:32
  104.3 17.4 %collective-permute-start.19 = (bf16[160,1152]{1,0:T(8,128)(2,1)S(1)}, bf16[160,1152]{1,0:T(8,128)(2,1)S(1)}, u32[]{:S(2)}, u32[]{:S(2)}) collective-permute-start(bf16[160,1152]{1,0:T(8,128)(2,1)S(1)} %get-tuple-element.49), channel_id=1, source_target_pairs={{0,4},{1,5},{2,6},{3,7},{4,0},{5,1},{6,2},{7,3},{8,12},{9,13},{10,... | collective-permute-start | bytes 1105928 | tf_op jit(solution)/shard_map/ppermute | solution.py:32
  110.2 11.8 %collective-permute-start.24 = (bf16[128,1152]{1,0:T(8,128)(2,1)S(1)}, bf16[128,1152]{1,0:T(8,128)(2,1)S(1)}, u32[]{:S(2)}, u32[]{:S(2)}) collective-permute-start(bf16[128,1152]{1,0:T(8,128)(2,1)S(1)} %get-tuple-element.44), channel_id=1, source_target_pairs={{0,96},{1,97},{2,98},{3,99},{4,100},{5,101},{6,102},{7,103},{8,104... | collective-permute-start | bytes 884744 | tf_op jit(solution)/shard_map/ppermute | solution.py:32
  112.5 9.5 %collective-permute-start.23 = (bf16[128,1152]{1,0:T(8,128)(2,1)S(1)}, bf16[128,1152]{1,0:T(8,128)(2,1)S(1)}, u32[]{:S(2)}, u32[]{:S(2)}) collective-permute-start(bf16[128,1152]{1,0:T(8,128)(2,1)S(1)} %get-tuple-element.46), channel_id=1, source_target_pairs={{0,32},{1,33},{2,34},{3,35},{4,36},{5,37},{6,38},{7,39},{8,40},{9,... | collective-permute-start | bytes 884744 | tf_op jit(solution)/shard_map/ppermute | solution.py:32
  122.3 20.3 %collective-permute-start.26 = (bf16[256,1152]{1,0:T(8,128)(2,1)S(1)}, bf16[256,1152]{1,0:T(8,128)(2,1)S(1)}, u32[]{:S(2)}, u32[]{:S(2)}) collective-permute-start(bf16[256,1152]{1,0:T(8,128)(2,1)S(1)} %get-tuple-element.30), channel_id=1, source_target_pairs={{0,96},{1,97},{2,98},{3,99},{4,100},{5,101},{6,102},{7,103},{8,104... | collective-permute-start | bytes 1769480 | tf_op jit(solution)/shard_map/ppermute | solution.py:32
  122.3 20.2 %collective-permute-start.25 = (bf16[256,1152]{1,0:T(8,128)(2,1)S(1)}, bf16[256,1152]{1,0:T(8,128)(2,1)S(1)}, u32[]{:S(2)}, u32[]{:S(2)}) collective-permute-start(bf16[256,1152]{1,0:T(8,128)(2,1)S(1)} %get-tuple-element.29), channel_id=1, source_target_pairs={{0,32},{1,33},{2,34},{3,35},{4,36},{5,37},{6,38},{7,39},{8,40},{9,... | collective-permute-start | bytes 1769480 | tf_op jit(solution)/shard_map/ppermute | solution.py:32
  123.8 6.0 %collective-permute-start.27 = (bf16[80,1152]{1,0:T(8,128)(2,1)S(1)}, bf16[80,1152]{1,0:T(8,128)(2,1)S(1)}, u32[]{:S(2)}, u32[]{:S(2)}) collective-permute-start(bf16[80,1152]{1,0:T(8,128)(2,1)S(1)} %slice.361), channel_id=1, source_target_pairs={{0,1},{1,0},{2,3},{3,2},{4,5},{5,4},{6,7},{7,6},{8,9},{9,8},{10,11... | collective-permute-start | bytes 552968 | tf_op jit(solution)/shard_map/ppermute | solution.py:32
  127.2 7.6 %collective-permute-start.32 = (bf16[128,1152]{1,0:T(8,128)(2,1)S(1)}, bf16[128,1152]{1,0:T(8,128)(2,1)S(1)}, u32[]{:S(2)}, u32[]{:S(2)}) collective-permute-start(bf16[128,1152]{1,0:T(8,128)(2,1)S(1)} %get-tuple-element.53), channel_id=1, source_target_pairs={{0,6},{1,7},{2,0},{3,1},{4,2},{5,3},{6,4},{7,5},{8,14},{9,15},{10,... | collective-permute-start | bytes 884744 | tf_op jit(solution)/shard_map/ppermute | solution.py:32
  127.3 15.0 %collective-permute-start.31 = (bf16[128,1152]{1,0:T(8,128)(2,1)S(1)}, bf16[128,1152]{1,0:T(8,128)(2,1)S(1)}, u32[]{:S(2)}, u32[]{:S(2)}) collective-permute-start(bf16[128,1152]{1,0:T(8,128)(2,1)S(1)} %get-tuple-element.54), channel_id=1, source_target_pairs={{0,2},{1,3},{2,4},{3,5},{4,6},{5,7},{6,0},{7,1},{8,10},{9,11},{10,... | collective-permute-start | bytes 884744 | tf_op jit(solution)/shard_map/ppermute | solution.py:32
  129.8 12.5 %collective-permute-start.30 = (bf16[128,1152]{1,0:T(8,128)(2,1)S(1)}, bf16[128,1152]{1,0:T(8,128)(2,1)S(1)}, u32[]{:S(2)}, u32[]{:S(2)}) collective-permute-start(bf16[128,1152]{1,0:T(8,128)(2,1)S(1)} %get-tuple-element.52), channel_id=1, source_target_pairs={{0,4},{1,5},{2,6},{3,7},{4,0},{5,1},{6,2},{7,3},{8,12},{9,13},{10,... | collective-permute-start | bytes 884744 | tf_op jit(solution)/shard_map/ppermute | solution.py:32
  134.8 7.7 %collective-permute-start.28 = (bf16[80,1152]{1,0:T(8,128)(2,1)S(1)}, bf16[80,1152]{1,0:T(8,128)(2,1)S(1)}, u32[]{:S(2)}, u32[]{:S(2)}) collective-permute-start(bf16[80,1152]{1,0:T(8,128)(2,1)S(1)} %add_convert_fusion.4), channel_id=1, source_target_pairs={{0,16},{1,17},{2,18},{3,19},{4,20},{5,21},{6,22},{7,23},{8,24},{9,... | collective-permute-start | bytes 552968 | tf_op jit(solution)/shard_map/ppermute | solution.py:32
  143.0 6.0 %collective-permute-start.35 = (bf16[80,1152]{1,0:T(8,128)(2,1)S(1)}, bf16[80,1152]{1,0:T(8,128)(2,1)S(1)}, u32[]{:S(2)}, u32[]{:S(2)}) collective-permute-start(bf16[80,1152]{1,0:T(8,128)(2,1)S(1)} %add_convert_fusion.3), channel_id=1, source_target_pairs={{0,32},{1,33},{2,34},{3,35},{4,36},{5,37},{6,38},{7,39},{8,40},{9,... | collective-permute-start | bytes 552968 | tf_op jit(solution)/shard_map/ppermute | solution.py:32
  144.4 7.4 %collective-permute-start.34 = (bf16[80,1152]{1,0:T(8,128)(2,1)S(1)}, bf16[80,1152]{1,0:T(8,128)(2,1)S(1)}, u32[]{:S(2)}, u32[]{:S(2)}) collective-permute-start(bf16[80,1152]{1,0:T(8,128)(2,1)S(1)} %add_convert_fusion.3), channel_id=1, source_target_pairs={{0,64},{1,65},{2,66},{3,67},{4,68},{5,69},{6,70},{7,71},{8,72},{9,... | collective-permute-start | bytes 552968 | tf_op jit(solution)/shard_map/ppermute | solution.py:32
  144.4 11.1 %collective-permute-start.33 = (bf16[128,1152]{1,0:T(8,128)(2,1)S(1)}, bf16[128,1152]{1,0:T(8,128)(2,1)S(1)}, u32[]{:S(2)}, u32[]{:S(2)}) collective-permute-start(bf16[128,1152]{1,0:T(8,128)(2,1)S(1)} %slice.360), channel_id=1, source_target_pairs={{0,16},{1,17},{2,18},{3,19},{4,20},{5,21},{6,22},{7,23},{8,24},{9,... | collective-permute-start | bytes 884744 | tf_op jit(solution)/shard_map/ppermute | solution.py:32
  (26 other events, 137.9 us)

commit v2 on v0

--- a/solution.py
+++ b/solution.py
@@ -79,21 +79,31 @@
     return (lax.rem(x + dx, 4) * 2 + lax.rem(yh + dy, 2)) * 144
 
 
-def prepare_kernel(pos, weight, pooled, text, own, emb):
-    own[pl.ds(0, 80), :] = weight[pl.ds(pl.multiple_of(pos[2] * 64, 16), 80), :]
-    own[pl.ds(80, 128), :] = pooled[...]
-    values = text[...].astype(F32)
+def prepare_kernel(weight, pooled, text, own, emb, held, sems):
+    core = lax.rem(lax.axis_index("dp"), 2)
+    share = weight.at[pl.ds(pl.multiple_of(core * 64, 16), 80)]
+    copies = [
+        pltpu.make_async_copy(text, held, sems.at[0]),
+        pltpu.make_async_copy(share, own.at[pl.ds(0, 80)], sems.at[1]),
+        pltpu.make_async_copy(pooled, own.at[pl.ds(80, 128)], sems.at[2]),
+    ]
+    for copy in copies:
+        copy.start()
+    for copy in copies:
+        copy.wait()
+    values = held[...].astype(F32)
     emb[...] = (values / jnp.sqrt(jnp.sum(values * values, axis=-1, keepdims=True) + epsilon)).astype(BF)
 
 
-def prepare(pos, weight, pooled, text):
+def prepare(weight, pooled, text):
     return pl.pallas_call(
         prepare_kernel,
         out_shape=[jax.ShapeDtypeStruct((208, 1152), BF), jax.ShapeDtypeStruct((128, 1152), BF)],
-        in_specs=[pl.BlockSpec(memory_space=pltpu.SMEM)] + [pl.BlockSpec(memory_space=pltpu.VMEM)] * 3,
+        in_specs=[pl.BlockSpec(memory_space=pl.ANY)] * 3,
         out_specs=[pl.BlockSpec(memory_space=pltpu.VMEM)] * 2,
-        compiler_params=pltpu.CompilerParams(vmem_limit_bytes=32 * 2**20),
-    )(pos, weight, pooled, text)
+        scratch_shapes=[pltpu.VMEM((128, 1152), BF), pltpu.SemaphoreType.DMA((3,))],
+        compiler_params=pltpu.CompilerParams(vmem_limit_bytes=63 * 2**20),
+    )(weight, pooled, text)
 
 
 def assemble_kernel(pos, near, far, near_c, far_c, out):
@@ -144,7 +154,7 @@
     mult = logit_scale[0]
     bias = logit_bias[0]
 
-    own, text_emb = prepare(pos, out_weight, pooled, text_feats)
+    own, text_emb = prepare(out_weight, pooled, text_feats)
     oth = shift(own, "yh", 1)
     own_p, own_m = both_ways(own, "x")
     oth_p, oth_m = both_ways(oth, "x")

time: 161 us -> 160 us (level)
  waiting for transfers between devices: 57.5 us -> 54.8 us
    ppermute x38, waiting for transfers between devices: 57.5 us -> 54.8 us  [shift(): return lax.ppermute(value, AXES, pairs)]
  transfers between devices with their start and end apart: 38 -> 38, of which waited for: 16 -> 16; matrix products, arithmetic and copies ran while one was open for 20% -> 22% of each run, Pallas kernels for 0% -> 0%
where the time goes in v2:
time: 160 us; the launch traced here: 157 us
  waiting for transfers between devices  54.8 us (34%)
  starting transfers between devices  40.3 us (25%)
  matrix products  39.2 us (25%)
  other arithmetic  9.95 us (6%)
  local copies, waits for them, and re-layouts  5.98 us (4%)
  Pallas kernels  3.55 us (2%)
  between operations  2.96 us (2%)
    ppermute x38, waiting for transfers between devices, shift(): return lax.ppermute(value, AXES, pairs)  54.8 us
    ppermute x38, starting transfers between devices, shift(): return lax.ppermute(value, AXES, pairs)  40.3 us
    dot_general x4, matrix products, back_t(): lax.dot_general(pg, e, (((0,), (0,)), ((), ())), preferred_element_type=F32)  20.7 us
    dot_general x1, matrix products, pair(): lax.dot_general(e, t, (((1,), (1,)), ((), ())), preferred_element_type=F32)  6.92 us
    unnamed x58, local copies, waits for them, and re-layouts  5.2 us
    dot_general x1, matrix products, embed(): raw = jnp.dot(rows, weight, preferred_element_type=F32)  3.63 us
  transfers between devices with their start and end apart: 38, of which 16 were waited for; matrix products, arithmetic and copies ran while one was open for 22% of the time, Pallas kernels for 0%

profile of v2, /device:TPU:1, one launch (start us, length us, event | category | flops | bytes accessed | tf_op | source)
XLA Modules:
  0.0 156.7 jit_solution(1019580765310429730)
XLA Ops:
  0.6 2.0 %shard_map.76 = (bf16[208,1152]{1,0:T(8,128)(2,1)}, bf16[128,1152]{1,0:T(8,128)(2,1)}) custom-call(bf16[144,1152]{1,0:T(8,128)(2,1)} %weight.1, bf16[128,1152]{1,0:T(8,128)(2,1)} %pooled.1, bf16[128,1152]{1,0:T(8,128)(2,1)} %text.1), custom_call_target="tpu_custom_call" | custom-call | tf_op jit(solution)/shard_map/pallas_call | solution.py:99
  2.7 3.8 %collective-permute-start.2 = (bf16[208,1152]{1,0:T(8,128)(2,1)}, bf16[208,1152]{1,0:T(8,128)(2,1)S(1)}, u32[]{:S(2)}, u32[]{:S(2)}) collective-permute-start(bf16[208,1152]{1,0:T(8,128)(2,1)} %get-tuple-element.24), channel_id=1, source_target_pairs={{0,1},{1,0},{2,3},{3,2},{4,5},{5,4},{6,7},{7,6},{8,9},{9,8},{10,11... | collective-permute-start | bytes 1437704 | tf_op jit(solution)/shard_map/ppermute | solution.py:32
  7.7 1.5 collective-permute-start
  9.2 3.8 %collective-permute-start.10 = (bf16[128,1152]{1,0:T(8,128)(2,1)}, bf16[128,1152]{1,0:T(8,128)(2,1)S(1)}, u32[]{:S(2)}, u32[]{:S(2)}) collective-permute-start(bf16[128,1152]{1,0:T(8,128)(2,1)} %get-tuple-element.26), channel_id=1, source_target_pairs={{0,96},{1,97},{2,98},{3,99},{4,100},{5,101},{6,102},{7,103},{8,104... | collective-permute-start | bytes 884744 | tf_op jit(solution)/shard_map/ppermute | solution.py:32
  18.0 3.0 %collective-permute-done.12 = bf16[128,1152]{1,0:T(8,128)(2,1)S(1)} collective-permute-done((bf16[128,1152]{1,0:T(8,128)(2,1)}, bf16[128,1152]{1,0:T(8,128)(2,1)S(1)}, u32[]{:S(2)}, u32[]{:S(2)}) %collective-permute-start.12) | collective-permute-done | bytes 294944 | tf_op jit(solution)/shard_map/ppermute | solution.py:32
  23.3 3.5 %collective-permute-done.9 = bf16[128,1152]{1,0:T(8,128)(2,1)S(1)} collective-permute-done((bf16[128,1152]{1,0:T(8,128)(2,1)S(1)}, bf16[128,1152]{1,0:T(8,128)(2,1)S(1)}, u32[]{:S(2)}, u32[]{:S(2)}) %collective-permute-start.9) | collective-permute-done | bytes 294944 | tf_op jit(solution)/shard_map/ppermute | solution.py:32
  28.3 4.9 %collective-permute-done.3 = bf16[208,1152]{1,0:T(8,128)(2,1)S(1)} collective-permute-done((bf16[208,1152]{1,0:T(8,128)(2,1)S(1)}, bf16[208,1152]{1,0:T(8,128)(2,1)S(1)}, u32[]{:S(2)}, u32[]{:S(2)}) %collective-permute-start.3) | collective-permute-done | bytes 479264 | tf_op jit(solution)/shard_map/ppermute | solution.py:32
  33.5 2.7 %collective-permute-start.6 = (bf16[224,1152]{1,0:T(8,128)(2,1)S(1)}, bf16[224,1152]{1,0:T(8,128)(2,1)S(1)}, u32[]{:S(2)}, u32[]{:S(2)}) collective-permute-start(bf16[224,1152]{1,0:T(8,128)(2,1)S(1)} %pad_maximum_fusion.3), channel_id=1, source_target_pairs={{0,6},{1,7},{2,0},{3,1},{4,2},{5,3},{6,4},{7,5},{8,14},{9,15},{10,... | collective-permute-start | bytes 1548296 | tf_op jit(solution)/shard_map/ppermute | solution.py:32
  36.3 4.8 %collective-permute-start.7 = (bf16[480,1152]{1,0:T(8,128)(2,1)S(1)}, bf16[480,1152]{1,0:T(8,128)(2,1)S(1)}, u32[]{:S(2)}, u32[]{:S(2)}) collective-permute-start(bf16[480,1152]{1,0:T(8,128)(2,1)S(1)} %slice_dynamic-update-slice_fusion.18.near), channel_id=1, source_target_pairs={{0,8},{1,9},{2,10},{3,11},{4,12},{5,13},{6,14},{7,15},{8,0},{9,1},... | collective-permute-start | bytes 3317768 | tf_op jit(solution)/shard_map/ppermute | solution.py:32
  41.2 1.9 %collective-permute-start.15 = (bf16[128,1152]{1,0:T(8,128)(2,1)S(1)}, bf16[128,1152]{1,0:T(8,128)(2,1)S(1)}, u32[]{:S(2)}, u32[]{:S(2)}) collective-permute-start(bf16[128,1152]{1,0:T(8,128)(2,1)S(1)} %pad_maximum_fusion.6), channel_id=1, source_target_pairs={{0,96},{1,97},{2,98},{3,99},{4,100},{5,101},{6,102},{7,103},{8,104... | collective-permute-start | bytes 884744 | tf_op jit(solution)/shard_map/ppermute | solution.py:32
  43.4 6.5 %collective-permute-done.15 = bf16[128,1152]{1,0:T(8,128)(2,1)S(1)} collective-permute-done((bf16[128,1152]{1,0:T(8,128)(2,1)S(1)}, bf16[128,1152]{1,0:T(8,128)(2,1)S(1)}, u32[]{:S(2)}, u32[]{:S(2)}) %collective-permute-start.15) | collective-permute-done | bytes 294944 | tf_op jit(solution)/shard_map/ppermute | solution.py:32
  50.0 2.8 %collective-permute-done.14 = bf16[128,1152]{1,0:T(8,128)(2,1)S(1)} collective-permute-done((bf16[128,1152]{1,0:T(8,128)(2,1)S(1)}, bf16[128,1152]{1,0:T(8,128)(2,1)S(1)}, u32[]{:S(2)}, u32[]{:S(2)}) %collective-permute-start.14) | collective-permute-done | bytes 294944 | tf_op jit(solution)/shard_map/ppermute | solution.py:32
  57.1 3.6 %multiply_reduce_fusion = (f32[1024]{0:T(1024)S(1)}, f32[1024,1152]{1,0:T(8,128)S(1)}) fusion(bf16[1024,1152]{1,0:T(8,128)(2,1)S(1)} %get-tuple-element.67, bf16[1152,1152]{1,0:T(8,128)(2,1)S(1)} %shard_map.77), kind=kOutput, calls=%fused_computation.5 | convolution fusion | flops 2720267264 | bytes 9736192 | tf_op jit(solution)/shard_map/dot_general | solution.py:184
  61.6 6.9 %multiply_convert_fusion = bf16[1024,2048]{1,0:T(8,128)(2,1)S(1)} fusion(bf16[1024,1152]{1,0:T(8,128)(2,1)S(1)} %divide_convert_fusion, bf16[2048,1152]{1,0:T(8,128)(2,1)S(1)} %slice_dynamic-update-slice_fusion.2, f32[]{:T(128)} %bitcast.21, f32[]{:T(128)} %bitcast.19), kind=kOutput, calls=%fused_computation.1 | convolution fusion | flops 4846518272 | bytes 11272200 | tf_op jit(solution)/shard_map/dot_general | solution.py:191
  68.8 2.9 %fusion.13 = f32[512,1152]{1,0:T(8,128)S(1)} fusion(bf16[2048,1152]{1,0:T(8,128)(2,1)S(1)} %slice_dynamic-update-slice_fusion.2, bf16[1024,2048]{1,0:T(8,128)(2,1)S(1)} %fusion.26), kind=kOutput, calls=%fused_computation.25 | convolution fusion | flops 2415919104 | bytes 9175040 | tf_op jit(solution)/shard_map/dot_general | solution.py:208
  71.7 3.2 %fusion.5 = (f32[512]{0:T(512)S(1)}, f32[512]{0:T(512)S(1)}, f32[512,1152]{1,0:T(8,128)S(1)}) fusion(bf16[1024,1152]{1,0:T(8,128)(2,1)S(1)} %divide_convert_fusion, f32[512,1152]{1,0:T(8,128)S(1)} %fusion.13, bf16[2048,1152]{1,0:T(8,128)(2,1)S(1)} %slice_dynamic-update-slice_fusion.2, bf16[1024,2048]{1,0:T(8,128)(2,1)S(1)} %fusion.26), kind=kOutput, calls=%fused_computation.16 | convolution fusion | flops 2419457024 | bytes 13897728 | tf_op jit(solution)/shard_map/dot_general | solution.py:209
  75.9 1.7 %fusion.39 = f32[1152,1152]{1,0:T(8,128)S(1)} fusion(bf16[512,1152]{1,0:T(8,128)(2,1)S(1)} %get-tuple-element.69, bf16[512,1152]{1,0:T(8,128)(2,1)S(1)} %get-tuple-element.40), kind=kOutput, calls=%fused_computation.119 | convolution fusion | flops 1358954496 | bytes 7667712 | tf_op jit(solution)/shard_map/dot_general | solution.py:202
  77.7 1.7 %fusion.whole = bf16[1152,1152]{1,0:T(8,128)(2,1)S(1)} fusion(f32[1152,1152]{1,0:T(8,128)S(1)} %fusion.39, bf16[512,1152]{1,0:T(8,128)(2,1)S(1)} %get-tuple-element.66, bf16[512,1152]{1,0:T(8,128)(2,1)S(1)} %get-tuple-element.55), kind=kOutput, calls=%fused_computation.2 | convolution fusion | flops 1361608704 | bytes 10321920 | tf_op jit(solution)/shard_map/dot_general | solution.py:202
  80.7 14.2 %fusion.9 = bf16[1024,1152]{1,0:T(8,128)(2,1)} fusion(bf16[1024,1152]{1,0:T(8,128)(2,1)S(1)} %divide_convert_fusion, bf16[1024,2048]{1,0:T(8,128)(2,1)S(1)} %fusion.26), kind=kOutput, calls=%fused_computation.21 | convolution fusion | flops 2415919104 | bytes 6815744 | tf_op jit(solution)/shard_map/dot_general | solution.py:202
  96.4 2.7 %collective-permute-start.29 = (bf16[512,1152]{1,0:T(8,128)(2,1)}, bf16[512,1152]{1,0:T(8,128)(2,1)S(1)}, u32[]{:S(2)}, u32[]{:S(2)}) collective-permute-start(bf16[512,1152]{1,0:T(8,128)(2,1)} %copy-done.7), channel_id=1, source_target_pairs={{0,1},{1,0},{2,3},{3,2},{4,5},{5,4},{6,7},{7,6},{8,9},{9,8},{10,11... | collective-permute-start | bytes 3538952 | tf_op jit(solution)/shard_map/ppermute | solution.py:32
  99.1 2.2 %add_convert_fusion = bf16[640,1152]{1,0:T(8,128)(2,1)S(1)} fusion(bf16[640,1152]{1,0:T(8,128)(2,1)} %copy-done.9, bf16[640,1152]{1,0:T(8,128)(2,1)} %copy-done.2), kind=kLoop, calls=%fused_computation.6 | loop fusion | flops 2949120 | bytes 4423680 | tf_op jit(solution)/shard_map/convert_element_type | solution.py:219
  103.0 3.0 %fusion.15 = f32[1024,1152]{1,0:T(8,128)S(1)} fusion(bf16[1024,1152]{1,0:T(8,128)(2,1)S(1)} %copy-done.6, bf16[1024,2048]{1,0:T(8,128)(2,1)S(1)} %copy-done.15), kind=kOutput, calls=%fused_computation.27 | convolution fusion | flops 2415919104 | bytes 9175040 | tf_op jit(solution)/shard_map/dot_general | solution.py:202
  106.0 2.4 %fusion.32 = (bf16[1024,1152]{1,0:T(8,128)(2,1)S(1)}, f32[1024,1152]{1,0:T(8,128)S(1)}) fusion(f32[1024,1152]{1,0:T(8,128)S(1)} %fusion.15, bf16[1024,1152]{1,0:T(8,128)(2,1)} %collective-permute-done.22), kind=kLoop, calls=%fused_computation.112 | loop fusion | flops 3538944 | bytes 14155776 | tf_op jit(solution)/shard_map/convert.8
  108.6 2.6 %collective-permute-done.21 = bf16[160,1152]{1,0:T(8,128)(2,1)S(1)} collective-permute-done((bf16[160,1152]{1,0:T(8,128)(2,1)S(1)}, bf16[160,1152]{1,0:T(8,128)(2,1)S(1)}, u32[]{:S(2)}, u32[]{:S(2)}) %collective-permute-start.21) | collective-permute-done | bytes 368672 | tf_op jit(solution)/shard_map/ppermute | solution.py:32
  111.2 9.2 %collective-permute-done.20 = bf16[160,1152]{1,0:T(8,128)(2,1)S(1)} collective-permute-done((bf16[160,1152]{1,0:T(8,128)(2,1)S(1)}, bf16[160,1152]{1,0:T(8,128)(2,1)S(1)}, u32[]{:S(2)}, u32[]{:S(2)}) %collective-permute-start.20) | collective-permute-done | bytes 368672 | tf_op jit(solution)/shard_map/ppermute | solution.py:32
  123.0 2.6 %collective-permute-done.29 = bf16[512,1152]{1,0:T(8,128)(2,1)S(1)} collective-permute-done((bf16[512,1152]{1,0:T(8,128)(2,1)}, bf16[512,1152]{1,0:T(8,128)(2,1)S(1)}, u32[]{:S(2)}, u32[]{:S(2)}) %collective-permute-start.29) | collective-permute-done | bytes 1179680 | tf_op jit(solution)/shard_map/ppermute | solution.py:32
  129.8 3.7 %collective-permute-done.32 = bf16[128,1152]{1,0:T(8,128)(2,1)S(1)} collective-permute-done((bf16[128,1152]{1,0:T(8,128)(2,1)S(1)}, bf16[128,1152]{1,0:T(8,128)(2,1)S(1)}, u32[]{:S(2)}, u32[]{:S(2)}) %collective-permute-start.32) | collective-permute-done | bytes 294944 | tf_op jit(solution)/shard_map/ppermute | solution.py:32
  133.7 7.4 %collective-permute-done.31 = bf16[128,1152]{1,0:T(8,128)(2,1)S(1)} collective-permute-done((bf16[128,1152]{1,0:T(8,128)(2,1)S(1)}, bf16[128,1152]{1,0:T(8,128)(2,1)S(1)}, u32[]{:S(2)}, u32[]{:S(2)}) %collective-permute-start.31) | collective-permute-done | bytes 294944 | tf_op jit(solution)/shard_map/ppermute | solution.py:32
  143.2 1.6 %convolution_convert_fusion = bf16[128,1152]{1,0:T(8,128)(2,1)} fusion(bf16[128,1152]{1,0:T(8,128)(2,1)S(1)} %add_convert_fusion.2, bf16[1152,1152]{1,0:T(8,128)(2,1)S(1)} %shard_map.77), kind=kOutput, calls=%fused_computation.11 | convolution fusion | flops 339886080 | bytes 3244032 | tf_op jit(solution)/shard_map/dot_general | solution.py:242
  146.1 1.6 %collective-permute-done.35 = bf16[80,1152]{1,0:T(8,128)(2,1)S(1)} collective-permute-done((bf16[80,1152]{1,0:T(8,128)(2,1)S(1)}, bf16[80,1152]{1,0:T(8,128)(2,1)S(1)}, u32[]{:S(2)}, u32[]{:S(2)}) %collective-permute-start.35) | collective-permute-done | bytes 184352 | tf_op jit(solution)/shard_map/ppermute | solution.py:32
  147.7 2.9 %collective-permute-done.34 = bf16[80,1152]{1,0:T(8,128)(2,1)S(1)} collective-permute-done((bf16[80,1152]{1,0:T(8,128)(2,1)S(1)}, bf16[80,1152]{1,0:T(8,128)(2,1)S(1)}, u32[]{:S(2)}, u32[]{:S(2)}) %collective-permute-start.34) | collective-permute-done | bytes 184352 | tf_op jit(solution)/shard_map/ppermute | solution.py:32
  150.7 3.6 %collective-permute-start.37 = (bf16[80,1152]{1,0:T(8,128)(2,1)S(1)}, bf16[80,1152]{1,0:T(8,128)(2,1)S(1)}, u32[]{:S(2)}, u32[]{:S(2)}) collective-permute-start(bf16[80,1152]{1,0:T(8,128)(2,1)S(1)} %add_convert_fusion.3), channel_id=1, source_target_pairs={{0,8},{1,9},{2,10},{3,11},{4,12},{5,13},{6,14},{7,15},{8,0},{9,1},... | collective-permute-start | bytes 552968 | tf_op jit(solution)/shard_map/ppermute | solution.py:32
  (166 shorter events, 32.7 us)
Async XLA Ops:
  2.7 18.4 %collective-permute-start.2 = (bf16[208,1152]{1,0:T(8,128)(2,1)}, bf16[208,1152]{1,0:T(8,128)(2,1)S(1)}, u32[]{:S(2)}, u32[]{:S(2)}) collective-permute-start(bf16[208,1152]{1,0:T(8,128)(2,1)} %get-tuple-element.24), channel_id=1, source_target_pairs={{0,1},{1,0},{2,3},{3,2},{4,5},{5,4},{6,7},{7,6},{8,9},{9,8},{10,11... | collective-permute-start | bytes 1437704 | tf_op jit(solution)/shard_map/ppermute | solution.py:32
  6.5 16.7 %collective-permute-start.1 = (bf16[208,1152]{1,0:T(8,128)(2,1)}, bf16[208,1152]{1,0:T(8,128)(2,1)S(1)}, u32[]{:S(2)}, u32[]{:S(2)}) collective-permute-start(bf16[208,1152]{1,0:T(8,128)(2,1)} %get-tuple-element.24), channel_id=1, source_target_pairs={{0,2},{1,3},{2,4},{3,5},{4,6},{5,7},{6,0},{7,1},{8,10},{9,11},{10,... | collective-permute-start | bytes 1437704 | tf_op jit(solution)/shard_map/ppermute | solution.py:32
  7.7 15.3 %collective-permute-start = (bf16[208,1152]{1,0:T(8,128)(2,1)}, bf16[208,1152]{1,0:T(8,128)(2,1)S(1)}, u32[]{:S(2)}, u32[]{:S(2)}) collective-permute-start(bf16[208,1152]{1,0:T(8,128)(2,1)} %get-tuple-element.24), channel_id=1, source_target_pairs={{0,6},{1,7},{2,0},{3,1},{4,2},{5,3},{6,4},{7,5},{8,14},{9,15},{10,... | collective-permute-start | bytes 1437704 | tf_op jit(solution)/shard_map/ppermute | solution.py:32
  9.2 8.9 %collective-permute-start.10 = (bf16[128,1152]{1,0:T(8,128)(2,1)}, bf16[128,1152]{1,0:T(8,128)(2,1)S(1)}, u32[]{:S(2)}, u32[]{:S(2)}) collective-permute-start(bf16[128,1152]{1,0:T(8,128)(2,1)} %get-tuple-element.26), channel_id=1, source_target_pairs={{0,96},{1,97},{2,98},{3,99},{4,100},{5,101},{6,102},{7,103},{8,104... | collective-permute-start | bytes 884744 | tf_op jit(solution)/shard_map/ppermute | solution.py:32
  12.9 8.1 %collective-permute-start.12 = (bf16[128,1152]{1,0:T(8,128)(2,1)}, bf16[128,1152]{1,0:T(8,128)(2,1)S(1)}, u32[]{:S(2)}, u32[]{:S(2)}) collective-permute-start(bf16[128,1152]{1,0:T(8,128)(2,1)} %get-tuple-element.26), channel_id=1, source_target_pairs={{0,32},{1,33},{2,34},{3,35},{4,36},{5,37},{6,38},{7,39},{8,40},{9,... | collective-permute-start | bytes 884744 | tf_op jit(solution)/shard_map/ppermute | solution.py:32
  21.6 11.8 %collective-permute-start.5 = (bf16[208,1152]{1,0:T(8,128)(2,1)S(1)}, bf16[208,1152]{1,0:T(8,128)(2,1)S(1)}, u32[]{:S(2)}, u32[]{:S(2)}) collective-permute-start(bf16[208,1152]{1,0:T(8,128)(2,1)S(1)} %collective-permute-done.2), channel_id=1, source_target_pairs={{0,6},{1,7},{2,0},{3,1},{4,2},{5,3},{6,4},{7,5},{8,14},{9,15},{10,... | collective-permute-start | bytes 1437704 | tf_op jit(solution)/shard_map/ppermute | solution.py:32
  22.8 10.4 %collective-permute-start.3 = (bf16[208,1152]{1,0:T(8,128)(2,1)S(1)}, bf16[208,1152]{1,0:T(8,128)(2,1)S(1)}, u32[]{:S(2)}, u32[]{:S(2)}) collective-permute-start(bf16[208,1152]{1,0:T(8,128)(2,1)S(1)} %collective-permute-done.2), channel_id=1, source_target_pairs={{0,2},{1,3},{2,4},{3,5},{4,6},{5,7},{6,0},{7,1},{8,10},{9,11},{10,... | collective-permute-start | bytes 1437704 | tf_op jit(solution)/shard_map/ppermute | solution.py:32
  26.7 14.4 %collective-permute-start.11 = (bf16[128,1152]{1,0:T(8,128)(2,1)S(1)}, bf16[128,1152]{1,0:T(8,128)(2,1)S(1)}, u32[]{:S(2)}, u32[]{:S(2)}) collective-permute-start(bf16[128,1152]{1,0:T(8,128)(2,1)S(1)} %collective-permute-done.9), channel_id=1, source_target_pairs={{0,96},{1,97},{2,98},{3,99},{4,100},{5,101},{6,102},{7,103},{8,104... | collective-permute-start | bytes 884744 | tf_op jit(solution)/shard_map/ppermute | solution.py:32
  27.5 15.6 %collective-permute-start.13 = (bf16[128,1152]{1,0:T(8,128)(2,1)S(1)}, bf16[128,1152]{1,0:T(8,128)(2,1)S(1)}, u32[]{:S(2)}, u32[]{:S(2)}) collective-permute-start(bf16[128,1152]{1,0:T(8,128)(2,1)S(1)} %collective-permute-done.9), channel_id=1, source_target_pairs={{0,32},{1,33},{2,34},{3,35},{4,36},{5,37},{6,38},{7,39},{8,40},{9,... | collective-permute-start | bytes 884744 | tf_op jit(solution)/shard_map/ppermute | solution.py:32
  33.3 19.6 %collective-permute-start.4 = (bf16[192,1152]{1,0:T(8,128)(2,1)S(1)}, bf16[192,1152]{1,0:T(8,128)(2,1)S(1)}, u32[]{:S(2)}, u32[]{:S(2)}) collective-permute-start(bf16[192,1152]{1,0:T(8,128)(2,1)S(1)} %pad_maximum_fusion.4), channel_id=1, source_target_pairs={{0,2},{1,3},{2,4},{3,5},{4,6},{5,7},{6,0},{7,1},{8,10},{9,11},{10,... | collective-permute-start | bytes 1327112 | tf_op jit(solution)/shard_map/ppermute | solution.py:32
  33.5 20.6 %collective-permute-start.6 = (bf16[224,1152]{1,0:T(8,128)(2,1)S(1)}, bf16[224,1152]{1,0:T(8,128)(2,1)S(1)}, u32[]{:S(2)}, u32[]{:S(2)}) collective-permute-start(bf16[224,1152]{1,0:T(8,128)(2,1)S(1)} %pad_maximum_fusion.3), channel_id=1, source_target_pairs={{0,6},{1,7},{2,0},{3,1},{4,2},{5,3},{6,4},{7,5},{8,14},{9,15},{10,... | collective-permute-start | bytes 1548296 | tf_op jit(solution)/shard_map/ppermute | solution.py:32
  36.3 20.0 %collective-permute-start.7 = (bf16[480,1152]{1,0:T(8,128)(2,1)S(1)}, bf16[480,1152]{1,0:T(8,128)(2,1)S(1)}, u32[]{:S(2)}, u32[]{:S(2)}) collective-permute-start(bf16[480,1152]{1,0:T(8,128)(2,1)S(1)} %slice_dynamic-update-slice_fusion.18.near), channel_id=1, source_target_pairs={{0,8},{1,9},{2,10},{3,11},{4,12},{5,13},{6,14},{7,15},{8,0},{9,1},... | collective-permute-start | bytes 3317768 | tf_op jit(solution)/shard_map/ppermute | solution.py:32
  41.2 8.7 %collective-permute-start.15 = (bf16[128,1152]{1,0:T(8,128)(2,1)S(1)}, bf16[128,1152]{1,0:T(8,128)(2,1)S(1)}, u32[]{:S(2)}, u32[]{:S(2)}) collective-permute-start(bf16[128,1152]{1,0:T(8,128)(2,1)S(1)} %pad_maximum_fusion.6), channel_id=1, source_target_pairs={{0,96},{1,97},{2,98},{3,99},{4,100},{5,101},{6,102},{7,103},{8,104... | collective-permute-start | bytes 884744 | tf_op jit(solution)/shard_map/ppermute | solution.py:32
  43.2 9.6 %collective-permute-start.14 = (bf16[128,1152]{1,0:T(8,128)(2,1)S(1)}, bf16[128,1152]{1,0:T(8,128)(2,1)S(1)}, u32[]{:S(2)}, u32[]{:S(2)}) collective-permute-start(bf16[128,1152]{1,0:T(8,128)(2,1)S(1)} %pad_maximum_fusion.5), channel_id=1, source_target_pairs={{0,32},{1,33},{2,34},{3,35},{4,36},{5,37},{6,38},{7,39},{8,40},{9,... | collective-permute-start | bytes 884744 | tf_op jit(solution)/shard_map/ppermute | solution.py:32
  80.2 14.7 %collective-permute-start.18 = (bf16[640,1152]{1,0:T(8,128)(2,1)S(1)}, bf16[640,1152]{1,0:T(8,128)(2,1)S(1)}, u32[]{:S(2)}, u32[]{:S(2)}) collective-permute-start(bf16[640,1152]{1,0:T(8,128)(2,1)S(1)} %get-tuple-element.30), channel_id=1, source_target_pairs={{0,8},{1,9},{2,10},{3,11},{4,12},{5,13},{6,14},{7,15},{8,0},{9,1},... | collective-permute-start | bytes 4423688 | tf_op jit(solution)/shard_map/ppermute | solution.py:32
  96.0 10.0 %collective-permute-start.22 = (bf16[1024,1152]{1,0:T(8,128)(2,1)}, bf16[1024,1152]{1,0:T(8,128)(2,1)}, u32[]{:S(2)}, u32[]{:S(2)}) collective-permute-start(bf16[1024,1152]{1,0:T(8,128)(2,1)} %fusion.9), channel_id=1, source_target_pairs={{0,8},{1,9},{2,10},{3,11},{4,12},{5,13},{6,14},{7,15},{8,0},{9,1},... | collective-permute-start | bytes 7077896 | tf_op jit(solution)/shard_map/ppermute | solution.py:32
  96.4 29.2 %collective-permute-start.29 = (bf16[512,1152]{1,0:T(8,128)(2,1)}, bf16[512,1152]{1,0:T(8,128)(2,1)S(1)}, u32[]{:S(2)}, u32[]{:S(2)}) collective-permute-start(bf16[512,1152]{1,0:T(8,128)(2,1)} %copy-done.7), channel_id=1, source_target_pairs={{0,1},{1,0},{2,3},{3,2},{4,5},{5,4},{6,7},{7,6},{8,9},{9,8},{10,11... | collective-permute-start | bytes 3538952 | tf_op jit(solution)/shard_map/ppermute | solution.py:32
  101.4 9.7 %collective-permute-start.21 = (bf16[160,1152]{1,0:T(8,128)(2,1)S(1)}, bf16[160,1152]{1,0:T(8,128)(2,1)S(1)}, u32[]{:S(2)}, u32[]{:S(2)}) collective-permute-start(bf16[160,1152]{1,0:T(8,128)(2,1)S(1)} %get-tuple-element.58), channel_id=1, source_target_pairs={{0,6},{1,7},{2,0},{3,1},{4,2},{5,3},{6,4},{7,5},{8,14},{9,15},{10,... | collective-permute-start | bytes 1105928 | tf_op jit(solution)/shard_map/ppermute | solution.py:32
  101.5 18.9 %collective-permute-start.20 = (bf16[160,1152]{1,0:T(8,128)(2,1)S(1)}, bf16[160,1152]{1,0:T(8,128)(2,1)S(1)}, u32[]{:S(2)}, u32[]{:S(2)}) collective-permute-start(bf16[160,1152]{1,0:T(8,128)(2,1)S(1)} %get-tuple-element.59), channel_id=1, source_target_pairs={{0,2},{1,3},{2,4},{3,5},{4,6},{5,7},{6,0},{7,1},{8,10},{9,11},{10,... | collective-permute-start | bytes 1105928 | tf_op jit(solution)/shard_map/ppermute | solution.py:32
  102.9 17.4 %collective-permute-start.19 = (bf16[160,1152]{1,0:T(8,128)(2,1)S(1)}, bf16[160,1152]{1,0:T(8,128)(2,1)S(1)}, u32[]{:S(2)}, u32[]{:S(2)}) collective-permute-start(bf16[160,1152]{1,0:T(8,128)(2,1)S(1)} %get-tuple-element.57), channel_id=1, source_target_pairs={{0,4},{1,5},{2,6},{3,7},{4,0},{5,1},{6,2},{7,3},{8,12},{9,13},{10,... | collective-permute-start | bytes 1105928 | tf_op jit(solution)/shard_map/ppermute | solution.py:32
  108.5 12.1 %collective-permute-start.24 = (bf16[128,1152]{1,0:T(8,128)(2,1)S(1)}, bf16[128,1152]{1,0:T(8,128)(2,1)S(1)}, u32[]{:S(2)}, u32[]{:S(2)}) collective-permute-start(bf16[128,1152]{1,0:T(8,128)(2,1)S(1)} %get-tuple-element.52), channel_id=1, source_target_pairs={{0,96},{1,97},{2,98},{3,99},{4,100},{5,101},{6,102},{7,103},{8,104... | collective-permute-start | bytes 884744 | tf_op jit(solution)/shard_map/ppermute | solution.py:32
  111.2 9.5 %collective-permute-start.23 = (bf16[128,1152]{1,0:T(8,128)(2,1)S(1)}, bf16[128,1152]{1,0:T(8,128)(2,1)S(1)}, u32[]{:S(2)}, u32[]{:S(2)}) collective-permute-start(bf16[128,1152]{1,0:T(8,128)(2,1)S(1)} %get-tuple-element.54), channel_id=1, source_target_pairs={{0,32},{1,33},{2,34},{3,35},{4,36},{5,37},{6,38},{7,39},{8,40},{9,... | collective-permute-start | bytes 884744 | tf_op jit(solution)/shard_map/ppermute | solution.py:32
  120.9 20.4 %collective-permute-start.26 = (bf16[256,1152]{1,0:T(8,128)(2,1)S(1)}, bf16[256,1152]{1,0:T(8,128)(2,1)S(1)}, u32[]{:S(2)}, u32[]{:S(2)}) collective-permute-start(bf16[256,1152]{1,0:T(8,128)(2,1)S(1)} %get-tuple-element.38), channel_id=1, source_target_pairs={{0,96},{1,97},{2,98},{3,99},{4,100},{5,101},{6,102},{7,103},{8,104... | collective-permute-start | bytes 1769480 | tf_op jit(solution)/shard_map/ppermute | solution.py:32
  121.0 20.4 %collective-permute-start.25 = (bf16[256,1152]{1,0:T(8,128)(2,1)S(1)}, bf16[256,1152]{1,0:T(8,128)(2,1)S(1)}, u32[]{:S(2)}, u32[]{:S(2)}) collective-permute-start(bf16[256,1152]{1,0:T(8,128)(2,1)S(1)} %get-tuple-element.37), channel_id=1, source_target_pairs={{0,32},{1,33},{2,34},{3,35},{4,36},{5,37},{6,38},{7,39},{8,40},{9,... | collective-permute-start | bytes 1769480 | tf_op jit(solution)/shard_map/ppermute | solution.py:32
  122.5 6.0 %collective-permute-start.27 = (bf16[80,1152]{1,0:T(8,128)(2,1)S(1)}, bf16[80,1152]{1,0:T(8,128)(2,1)S(1)}, u32[]{:S(2)}, u32[]{:S(2)}) collective-permute-start(bf16[80,1152]{1,0:T(8,128)(2,1)S(1)} %slice.373), channel_id=1, source_target_pairs={{0,1},{1,0},{2,3},{3,2},{4,5},{5,4},{6,7},{7,6},{8,9},{9,8},{10,11... | collective-permute-start | bytes 552968 | tf_op jit(solution)/shard_map/ppermute | solution.py:32
  126.0 7.6 %collective-permute-start.32 = (bf16[128,1152]{1,0:T(8,128)(2,1)S(1)}, bf16[128,1152]{1,0:T(8,128)(2,1)S(1)}, u32[]{:S(2)}, u32[]{:S(2)}) collective-permute-start(bf16[128,1152]{1,0:T(8,128)(2,1)S(1)} %get-tuple-element.61), channel_id=1, source_target_pairs={{0,6},{1,7},{2,0},{3,1},{4,2},{5,3},{6,4},{7,5},{8,14},{9,15},{10,... | collective-permute-start | bytes 884744 | tf_op jit(solution)/shard_map/ppermute | solution.py:32
  126.1 15.0 %collective-permute-start.31 = (bf16[128,1152]{1,0:T(8,128)(2,1)S(1)}, bf16[128,1152]{1,0:T(8,128)(2,1)S(1)}, u32[]{:S(2)}, u32[]{:S(2)}) collective-permute-start(bf16[128,1152]{1,0:T(8,128)(2,1)S(1)} %get-tuple-element.62), channel_id=1, source_target_pairs={{0,2},{1,3},{2,4},{3,5},{4,6},{5,7},{6,0},{7,1},{8,10},{9,11},{10,... | collective-permute-start | bytes 884744 | tf_op jit(solution)/shard_map/ppermute | solution.py:32
  128.4 12.7 %collective-permute-start.30 = (bf16[128,1152]{1,0:T(8,128)(2,1)S(1)}, bf16[128,1152]{1,0:T(8,128)(2,1)S(1)}, u32[]{:S(2)}, u32[]{:S(2)}) collective-permute-start(bf16[128,1152]{1,0:T(8,128)(2,1)S(1)} %get-tuple-element.60), channel_id=1, source_target_pairs={{0,4},{1,5},{2,6},{3,7},{4,0},{5,1},{6,2},{7,3},{8,12},{9,13},{10,... | collective-permute-start | bytes 884744 | tf_op jit(solution)/shard_map/ppermute | solution.py:32
  133.5 7.7 %collective-permute-start.28 = (bf16[80,1152]{1,0:T(8,128)(2,1)S(1)}, bf16[80,1152]{1,0:T(8,128)(2,1)S(1)}, u32[]{:S(2)}, u32[]{:S(2)}) collective-permute-start(bf16[80,1152]{1,0:T(8,128)(2,1)S(1)} %add_convert_fusion.5), channel_id=1, source_target_pairs={{0,16},{1,17},{2,18},{3,19},{4,20},{5,21},{6,22},{7,23},{8,24},{9,... | collective-permute-start | bytes 552968 | tf_op jit(solution)/shard_map/ppermute | solution.py:32
  141.7 6.0 %collective-permute-start.35 = (bf16[80,1152]{1,0:T(8,128)(2,1)S(1)}, bf16[80,1152]{1,0:T(8,128)(2,1)S(1)}, u32[]{:S(2)}, u32[]{:S(2)}) collective-permute-start(bf16[80,1152]{1,0:T(8,128)(2,1)S(1)} %add_convert_fusion.4), channel_id=1, source_target_pairs={{0,32},{1,33},{2,34},{3,35},{4,36},{5,37},{6,38},{7,39},{8,40},{9,... | collective-permute-start | bytes 552968 | tf_op jit(solution)/shard_map/ppermute | solution.py:32
  143.2 7.4 %collective-permute-start.34 = (bf16[80,1152]{1,0:T(8,128)(2,1)S(1)}, bf16[80,1152]{1,0:T(8,128)(2,1)S(1)}, u32[]{:S(2)}, u32[]{:S(2)}) collective-permute-start(bf16[80,1152]{1,0:T(8,128)(2,1)S(1)} %add_convert_fusion.4), channel_id=1, source_target_pairs={{0,64},{1,65},{2,66},{3,67},{4,68},{5,69},{6,70},{7,71},{8,72},{9,... | collective-permute-start | bytes 552968 | tf_op jit(solution)/shard_map/ppermute | solution.py:32
  143.2 11.2 %collective-permute-start.33 = (bf16[128,1152]{1,0:T(8,128)(2,1)S(1)}, bf16[128,1152]{1,0:T(8,128)(2,1)S(1)}, u32[]{:S(2)}, u32[]{:S(2)}) collective-permute-start(bf16[128,1152]{1,0:T(8,128)(2,1)S(1)} %slice.372), channel_id=1, source_target_pairs={{0,16},{1,17},{2,18},{3,19},{4,20},{5,21},{6,22},{7,23},{8,24},{9,... | collective-permute-start | bytes 884744 | tf_op jit(solution)/shard_map/ppermute | solution.py:32
  (24 other events, 197.7 us)

commit v3 on v1

--- a/solution.py
+++ b/solution.py
@@ -79,21 +79,31 @@
     return (lax.rem(x + dx, 4) * 2 + lax.rem(yh + dy, 2)) * 144
 
 
-def prepare_kernel(pos, weight, pooled, text, own, emb):
-    own[pl.ds(0, 80), :] = weight[pl.ds(pl.multiple_of(pos[2] * 64, 16), 80), :]
-    own[pl.ds(80, 128), :] = pooled[...]
-    values = text[...].astype(F32)
+def prepare_kernel(weight, pooled, text, own, emb, held, sems):
+    core = lax.rem(lax.axis_index("dp"), 2)
+    share = weight.at[pl.ds(pl.multiple_of(core * 64, 16), 80)]
+    copies = [
+        pltpu.make_async_copy(text, held, sems.at[0]),
+        pltpu.make_async_copy(share, own.at[pl.ds(0, 80)], sems.at[1]),
+        pltpu.make_async_copy(pooled, own.at[pl.ds(80, 128)], sems.at[2]),
+    ]
+    for copy in copies:
+        copy.start()
+    for copy in copies:
+        copy.wait()
+    values = held[...].astype(F32)
     emb[...] = (values / jnp.sqrt(jnp.sum(values * values, axis=-1, keepdims=True) + epsilon)).astype(BF)
 
 
-def prepare(pos, weight, pooled, text):
+def prepare(weight, pooled, text):
     return pl.pallas_call(
         prepare_kernel,
         out_shape=[jax.ShapeDtypeStruct((208, 1152), BF), jax.ShapeDtypeStruct((128, 1152), BF)],
-        in_specs=[pl.BlockSpec(memory_space=pltpu.SMEM)] + [pl.BlockSpec(memory_space=pltpu.VMEM)] * 3,
+        in_specs=[pl.BlockSpec(memory_space=pl.ANY)] * 3,
         out_specs=[pl.BlockSpec(memory_space=pltpu.VMEM)] * 2,
-        compiler_params=pltpu.CompilerParams(vmem_limit_bytes=32 * 2**20),
-    )(pos, weight, pooled, text)
+        scratch_shapes=[pltpu.VMEM((128, 1152), BF), pltpu.SemaphoreType.DMA((3,))],
+        compiler_params=pltpu.CompilerParams(vmem_limit_bytes=63 * 2**20),
+    )(weight, pooled, text)
 
 
 def assemble_kernel(pos, near, far, near_c, far_c, out):
@@ -151,7 +161,7 @@
     mult = logit_scale[0]
     bias = logit_bias[0]
 
-    own, text_emb = prepare(pos, out_weight, pooled, text_feats)
+    own, text_emb = prepare(out_weight, pooled, text_feats)
     oth = shift(own, "yh", 1)
     own_p, own_m = both_ways(own, "x")
     oth_p, oth_m = both_ways(oth, "x")
@@ -172,7 +182,7 @@
     fb = shift(jnp.concatenate([t_p[64:], u_p[64:]], 0), "z", -1)
     t_near = jnp.concatenate([text_emb, text_oth, t_p, u_p, t_m, u_m], 0)
     t_far = jnp.concatenate([fa[:64], fb[:64], fa[64:], fb[64:]], 0)
-    t_far, _ = join(t_far, w_far_c)
+    t_near, t_far, _ = join(t_near, t_far, w_far_c)
     c_near = shift(t_near, "c", 1)
     c_far = shift(t_far, "c", 1)
     texts = jnp.concatenate([t_near[:512], t_far, t_near[512:], c_near[:512], c_far, c_near[512:]], 0)

time: 161 us -> 159 us (0.988)
  waiting for transfers between devices: 57 us -> 54.2 us
    ppermute x38, waiting for transfers between devices: 57 us -> 54.2 us  [shift(): return lax.ppermute(value, AXES, pairs)]
    unnamed x60 -> x58, local copies, waits for them, and re-layouts: 6.93 us -> 6.94 us
  transfers between devices with their start and end apart: 38 -> 38, of which waited for: 16 -> 16; matrix products, arithmetic and copies ran while one was open for 19% -> 21% of each run, Pallas kernels for 1% -> 1%
where the time goes in v3:
time: 159 us; the launch traced here: 156 us
  waiting for transfers between devices  54.2 us (34%)
  starting transfers between devices  40.4 us (25%)
  matrix products  39.1 us (25%)
  local copies, waits for them, and re-layouts  7.72 us (5%)
  other arithmetic  7.67 us (5%)
  Pallas kernels  4.33 us (3%)
  between operations  2.94 us (2%)
    ppermute x38, waiting for transfers between devices, shift(): return lax.ppermute(value, AXES, pairs)  54.2 us
    ppermute x38, starting transfers between devices, shift(): return lax.ppermute(value, AXES, pairs)  40.4 us
    dot_general x4, matrix products, back_t(): lax.dot_general(pg, e, (((0,), (0,)), ((), ())), preferred_element_type=F32)  20.6 us
    unnamed x58, local copies, waits for them, and re-layouts  6.94 us
    dot_general x1, matrix products, pair(): lax.dot_general(e, t, (((1,), (1,)), ((), ())), preferred_element_type=F32)  6.94 us
    dot_general x1, matrix products, embed(): raw = jnp.dot(rows, weight, preferred_element_type=F32)  3.62 us
  transfers between devices with their start and end apart: 38, of which 16 were waited for; matrix products, arithmetic and copies ran while one was open for 21% of the time, Pallas kernels for 1%

profile of v3, /device:TPU:1, one launch (start us, length us, event | category | flops | bytes accessed | tf_op | source)
XLA Modules:
  0.0 156.4 jit_solution(2049222143239610934)
XLA Ops:
  0.6 2.0 %shard_map.76 = (bf16[208,1152]{1,0:T(8,128)(2,1)}, bf16[128,1152]{1,0:T(8,128)(2,1)}) custom-call(bf16[144,1152]{1,0:T(8,128)(2,1)} %weight.1, bf16[128,1152]{1,0:T(8,128)(2,1)} %pooled.1, bf16[128,1152]{1,0:T(8,128)(2,1)} %text.1), custom_call_target="tpu_custom_call" | custom-call | tf_op jit(solution)/shard_map/pallas_call | solution.py:99
  2.7 3.8 %collective-permute-start.2 = (bf16[208,1152]{1,0:T(8,128)(2,1)}, bf16[208,1152]{1,0:T(8,128)(2,1)S(1)}, u32[]{:S(2)}, u32[]{:S(2)}) collective-permute-start(bf16[208,1152]{1,0:T(8,128)(2,1)} %get-tuple-element.21), channel_id=1, source_target_pairs={{0,1},{1,0},{2,3},{3,2},{4,5},{5,4},{6,7},{7,6},{8,9},{9,8},{10,11... | collective-permute-start | bytes 1437704 | tf_op jit(solution)/shard_map/ppermute | solution.py:32
  7.7 1.5 collective-permute-start
  9.2 3.8 %collective-permute-start.10 = (bf16[128,1152]{1,0:T(8,128)(2,1)}, bf16[128,1152]{1,0:T(8,128)(2,1)S(1)}, u32[]{:S(2)}, u32[]{:S(2)}) collective-permute-start(bf16[128,1152]{1,0:T(8,128)(2,1)} %get-tuple-element.23), channel_id=1, source_target_pairs={{0,96},{1,97},{2,98},{3,99},{4,100},{5,101},{6,102},{7,103},{8,104... | collective-permute-start | bytes 884744 | tf_op jit(solution)/shard_map/ppermute | solution.py:32
  18.0 3.0 %collective-permute-done.12 = bf16[128,1152]{1,0:T(8,128)(2,1)S(1)} collective-permute-done((bf16[128,1152]{1,0:T(8,128)(2,1)}, bf16[128,1152]{1,0:T(8,128)(2,1)S(1)}, u32[]{:S(2)}, u32[]{:S(2)}) %collective-permute-start.12) | collective-permute-done | bytes 294944 | tf_op jit(solution)/shard_map/ppermute | solution.py:32
  23.3 3.5 %collective-permute-done.9 = bf16[128,1152]{1,0:T(8,128)(2,1)S(1)} collective-permute-done((bf16[128,1152]{1,0:T(8,128)(2,1)S(1)}, bf16[128,1152]{1,0:T(8,128)(2,1)S(1)}, u32[]{:S(2)}, u32[]{:S(2)}) %collective-permute-start.9) | collective-permute-done | bytes 294944 | tf_op jit(solution)/shard_map/ppermute | solution.py:32
  28.3 4.9 %collective-permute-done.3 = bf16[208,1152]{1,0:T(8,128)(2,1)S(1)} collective-permute-done((bf16[208,1152]{1,0:T(8,128)(2,1)S(1)}, bf16[208,1152]{1,0:T(8,128)(2,1)S(1)}, u32[]{:S(2)}, u32[]{:S(2)}) %collective-permute-start.3) | collective-permute-done | bytes 479264 | tf_op jit(solution)/shard_map/ppermute | solution.py:32
  33.5 2.7 %collective-permute-start.6 = (bf16[224,1152]{1,0:T(8,128)(2,1)S(1)}, bf16[224,1152]{1,0:T(8,128)(2,1)S(1)}, u32[]{:S(2)}, u32[]{:S(2)}) collective-permute-start(bf16[224,1152]{1,0:T(8,128)(2,1)S(1)} %pad_maximum_fusion.3), channel_id=1, source_target_pairs={{0,6},{1,7},{2,0},{3,1},{4,2},{5,3},{6,4},{7,5},{8,14},{9,15},{10,... | collective-permute-start | bytes 1548296 | tf_op jit(solution)/shard_map/ppermute | solution.py:32
  36.3 4.8 %collective-permute-start.7 = (bf16[480,1152]{1,0:T(8,128)(2,1)S(1)}, bf16[480,1152]{1,0:T(8,128)(2,1)S(1)}, u32[]{:S(2)}, u32[]{:S(2)}) collective-permute-start(bf16[480,1152]{1,0:T(8,128)(2,1)S(1)} %slice_dynamic-update-slice_fusion.18.near), channel_id=1, source_target_pairs={{0,8},{1,9},{2,10},{3,11},{4,12},{5,13},{6,14},{7,15},{8,0},{9,1},... | collective-permute-start | bytes 3317768 | tf_op jit(solution)/shard_map/ppermute | solution.py:32
  41.2 1.9 %collective-permute-start.15 = (bf16[128,1152]{1,0:T(8,128)(2,1)S(1)}, bf16[128,1152]{1,0:T(8,128)(2,1)S(1)}, u32[]{:S(2)}, u32[]{:S(2)}) collective-permute-start(bf16[128,1152]{1,0:T(8,128)(2,1)S(1)} %pad_maximum_fusion.6), channel_id=1, source_target_pairs={{0,96},{1,97},{2,98},{3,99},{4,100},{5,101},{6,102},{7,103},{8,104... | collective-permute-start | bytes 884744 | tf_op jit(solution)/shard_map/ppermute | solution.py:32
  43.4 6.5 %collective-permute-done.15 = bf16[128,1152]{1,0:T(8,128)(2,1)S(1)} collective-permute-done((bf16[128,1152]{1,0:T(8,128)(2,1)S(1)}, bf16[128,1152]{1,0:T(8,128)(2,1)S(1)}, u32[]{:S(2)}, u32[]{:S(2)}) %collective-permute-start.15) | collective-permute-done | bytes 294944 | tf_op jit(solution)/shard_map/ppermute | solution.py:32
  50.0 2.8 %collective-permute-done.14 = bf16[128,1152]{1,0:T(8,128)(2,1)S(1)} collective-permute-done((bf16[128,1152]{1,0:T(8,128)(2,1)S(1)}, bf16[128,1152]{1,0:T(8,128)(2,1)S(1)}, u32[]{:S(2)}, u32[]{:S(2)}) %collective-permute-start.14) | collective-permute-done | bytes 294944 | tf_op jit(solution)/shard_map/ppermute | solution.py:32
  57.0 3.6 %multiply_reduce_fusion = (f32[1024]{0:T(1024)S(1)}, f32[1024,1152]{1,0:T(8,128)S(1)}) fusion(bf16[1024,1152]{1,0:T(8,128)(2,1)S(1)} %get-tuple-element.61, bf16[1152,1152]{1,0:T(8,128)(2,1)S(1)} %shard_map.77), kind=kOutput, calls=%fused_computation.5 | convolution fusion | flops 2720267264 | bytes 9736192 | tf_op jit(solution)/shard_map/dot_general | solution.py:191
  61.6 6.9 %multiply_convert_fusion = bf16[1024,2048]{1,0:T(8,128)(2,1)S(1)} fusion(bf16[1024,1152]{1,0:T(8,128)(2,1)S(1)} %divide_convert_fusion, bf16[2048,1152]{1,0:T(8,128)(2,1)S(1)} %slice_dynamic-update-slice_fusion.2, f32[]{:T(128)} %bitcast.21, f32[]{:T(128)} %bitcast.19), kind=kOutput, calls=%fused_computation.1 | convolution fusion | flops 4846518272 | bytes 11272200 | tf_op jit(solution)/shard_map/dot_general | solution.py:198
  68.8 2.9 %fusion.13 = f32[512,1152]{1,0:T(8,128)S(1)} fusion(bf16[2048,1152]{1,0:T(8,128)(2,1)S(1)} %slice_dynamic-update-slice_fusion.2, bf16[1024,2048]{1,0:T(8,128)(2,1)S(1)} %fusion.26), kind=kOutput, calls=%fused_computation.24 | convolution fusion | flops 2415919104 | bytes 9175040 | tf_op jit(solution)/shard_map/dot_general | solution.py:215
  71.7 3.1 %fusion.5 = (f32[512]{0:T(512)S(1)}, f32[512]{0:T(512)S(1)}, f32[512,1152]{1,0:T(8,128)S(1)}) fusion(bf16[1024,1152]{1,0:T(8,128)(2,1)S(1)} %divide_convert_fusion, f32[512,1152]{1,0:T(8,128)S(1)} %fusion.13, bf16[2048,1152]{1,0:T(8,128)(2,1)S(1)} %slice_dynamic-update-slice_fusion.2, bf16[1024,2048]{1,0:T(8,128)(2,1)S(1)} %fusion.26), kind=kOutput, calls=%fused_computation.15 | convolution fusion | flops 2419457024 | bytes 13897728 | tf_op jit(solution)/shard_map/dot_general | solution.py:216
  75.8 1.7 %fusion.39 = f32[1152,1152]{1,0:T(8,128)S(1)} fusion(bf16[512,1152]{1,0:T(8,128)(2,1)S(1)} %get-tuple-element.63, bf16[512,1152]{1,0:T(8,128)(2,1)S(1)} %get-tuple-element.34), kind=kOutput, calls=%fused_computation.118 | convolution fusion | flops 1358954496 | bytes 7667712 | tf_op jit(solution)/shard_map/dot_general | solution.py:209
  77.6 1.7 %fusion.whole = bf16[1152,1152]{1,0:T(8,128)(2,1)S(1)} fusion(f32[1152,1152]{1,0:T(8,128)S(1)} %fusion.39, bf16[512,1152]{1,0:T(8,128)(2,1)S(1)} %get-tuple-element.60, bf16[512,1152]{1,0:T(8,128)(2,1)S(1)} %get-tuple-element.49), kind=kOutput, calls=%fused_computation.2 | convolution fusion | flops 1361608704 | bytes 10321920 | tf_op jit(solution)/shard_map/dot_general | solution.py:209
  80.5 14.1 %fusion.9 = bf16[1024,1152]{1,0:T(8,128)(2,1)} fusion(bf16[1024,1152]{1,0:T(8,128)(2,1)S(1)} %divide_convert_fusion, bf16[1024,2048]{1,0:T(8,128)(2,1)S(1)} %fusion.26), kind=kOutput, calls=%fused_computation.20 | convolution fusion | flops 2415919104 | bytes 6815744 | tf_op jit(solution)/shard_map/dot_general | solution.py:209
  96.2 2.7 %collective-permute-start.29 = (bf16[512,1152]{1,0:T(8,128)(2,1)}, bf16[512,1152]{1,0:T(8,128)(2,1)S(1)}, u32[]{:S(2)}, u32[]{:S(2)}) collective-permute-start(bf16[512,1152]{1,0:T(8,128)(2,1)} %copy-done.8), channel_id=1, source_target_pairs={{0,1},{1,0},{2,3},{3,2},{4,5},{5,4},{6,7},{7,6},{8,9},{9,8},{10,11... | collective-permute-start | bytes 3538952 | tf_op jit(solution)/shard_map/ppermute | solution.py:32
  101.3 1.5 collective-permute-start.20
  103.2 3.0 %fusion.15 = f32[1024,1152]{1,0:T(8,128)S(1)} fusion(bf16[1024,1152]{1,0:T(8,128)(2,1)S(1)} %copy-done.7, bf16[1024,2048]{1,0:T(8,128)(2,1)S(1)} %copy-done.15), kind=kOutput, calls=%fused_computation.26 | convolution fusion | flops 2415919104 | bytes 9175040 | tf_op jit(solution)/shard_map/dot_general | solution.py:209
  106.2 2.4 %fusion.32 = (bf16[1024,1152]{1,0:T(8,128)(2,1)S(1)}, f32[1024,1152]{1,0:T(8,128)S(1)}) fusion(f32[1024,1152]{1,0:T(8,128)S(1)} %fusion.15, bf16[1024,1152]{1,0:T(8,128)(2,1)} %collective-permute-done.22), kind=kLoop, calls=%fused_computation.111 | loop fusion | flops 3538944 | bytes 14155776 | tf_op jit(solution)/shard_map/convert.8
  108.7 2.2 %collective-permute-done.21 = bf16[160,1152]{1,0:T(8,128)(2,1)S(1)} collective-permute-done((bf16[160,1152]{1,0:T(8,128)(2,1)S(1)}, bf16[160,1152]{1,0:T(8,128)(2,1)S(1)}, u32[]{:S(2)}, u32[]{:S(2)}) %collective-permute-start.21) | collective-permute-done | bytes 368672 | tf_op jit(solution)/shard_map/ppermute | solution.py:32
  111.0 9.2 %collective-permute-done.20 = bf16[160,1152]{1,0:T(8,128)(2,1)S(1)} collective-permute-done((bf16[160,1152]{1,0:T(8,128)(2,1)S(1)}, bf16[160,1152]{1,0:T(8,128)(2,1)S(1)}, u32[]{:S(2)}, u32[]{:S(2)}) %collective-permute-start.20) | collective-permute-done | bytes 368672 | tf_op jit(solution)/shard_map/ppermute | solution.py:32
  122.7 2.6 %collective-permute-done.29 = bf16[512,1152]{1,0:T(8,128)(2,1)S(1)} collective-permute-done((bf16[512,1152]{1,0:T(8,128)(2,1)}, bf16[512,1152]{1,0:T(8,128)(2,1)S(1)}, u32[]{:S(2)}, u32[]{:S(2)}) %collective-permute-start.29) | collective-permute-done | bytes 1179680 | tf_op jit(solution)/shard_map/ppermute | solution.py:32
  129.7 3.6 %collective-permute-done.32 = bf16[128,1152]{1,0:T(8,128)(2,1)S(1)} collective-permute-done((bf16[128,1152]{1,0:T(8,128)(2,1)S(1)}, bf16[128,1152]{1,0:T(8,128)(2,1)S(1)}, u32[]{:S(2)}, u32[]{:S(2)}) %collective-permute-start.32) | collective-permute-done | bytes 294944 | tf_op jit(solution)/shard_map/ppermute | solution.py:32
  133.4 7.3 %collective-permute-done.31 = bf16[128,1152]{1,0:T(8,128)(2,1)S(1)} collective-permute-done((bf16[128,1152]{1,0:T(8,128)(2,1)S(1)}, bf16[128,1152]{1,0:T(8,128)(2,1)S(1)}, u32[]{:S(2)}, u32[]{:S(2)}) %collective-permute-start.31) | collective-permute-done | bytes 294944 | tf_op jit(solution)/shard_map/ppermute | solution.py:32
  143.0 1.6 %convolution_convert_fusion = bf16[128,1152]{1,0:T(8,128)(2,1)} fusion(bf16[128,1152]{1,0:T(8,128)(2,1)S(1)} %add_convert_fusion.1, bf16[1152,1152]{1,0:T(8,128)(2,1)S(1)} %copy-done.1), kind=kOutput, calls=%fused_computation.10 | convolution fusion | flops 339886080 | bytes 3244032 | tf_op jit(solution)/shard_map/dot_general | solution.py:248
  145.8 1.6 %collective-permute-done.35 = bf16[80,1152]{1,0:T(8,128)(2,1)S(1)} collective-permute-done((bf16[80,1152]{1,0:T(8,128)(2,1)S(1)}, bf16[80,1152]{1,0:T(8,128)(2,1)S(1)}, u32[]{:S(2)}, u32[]{:S(2)}) %collective-permute-start.35) | collective-permute-done | bytes 184352 | tf_op jit(solution)/shard_map/ppermute | solution.py:32
  147.4 2.9 %collective-permute-done.34 = bf16[80,1152]{1,0:T(8,128)(2,1)S(1)} collective-permute-done((bf16[80,1152]{1,0:T(8,128)(2,1)S(1)}, bf16[80,1152]{1,0:T(8,128)(2,1)S(1)}, u32[]{:S(2)}, u32[]{:S(2)}) %collective-permute-start.34) | collective-permute-done | bytes 184352 | tf_op jit(solution)/shard_map/ppermute | solution.py:32
  150.4 3.6 %collective-permute-start.37 = (bf16[80,1152]{1,0:T(8,128)(2,1)S(1)}, bf16[80,1152]{1,0:T(8,128)(2,1)S(1)}, u32[]{:S(2)}, u32[]{:S(2)}) collective-permute-start(bf16[80,1152]{1,0:T(8,128)(2,1)S(1)} %add_convert_fusion.2), channel_id=1, source_target_pairs={{0,8},{1,9},{2,10},{3,11},{4,12},{5,13},{6,14},{7,15},{8,0},{9,1},... | collective-permute-start | bytes 552968 | tf_op jit(solution)/shard_map/ppermute | solution.py:32
  (166 shorter events, 33.7 us)
Async XLA Ops:
  2.7 18.4 %collective-permute-start.2 = (bf16[208,1152]{1,0:T(8,128)(2,1)}, bf16[208,1152]{1,0:T(8,128)(2,1)S(1)}, u32[]{:S(2)}, u32[]{:S(2)}) collective-permute-start(bf16[208,1152]{1,0:T(8,128)(2,1)} %get-tuple-element.21), channel_id=1, source_target_pairs={{0,1},{1,0},{2,3},{3,2},{4,5},{5,4},{6,7},{7,6},{8,9},{9,8},{10,11... | collective-permute-start | bytes 1437704 | tf_op jit(solution)/shard_map/ppermute | solution.py:32
  6.5 16.7 %collective-permute-start.1 = (bf16[208,1152]{1,0:T(8,128)(2,1)}, bf16[208,1152]{1,0:T(8,128)(2,1)S(1)}, u32[]{:S(2)}, u32[]{:S(2)}) collective-permute-start(bf16[208,1152]{1,0:T(8,128)(2,1)} %get-tuple-element.21), channel_id=1, source_target_pairs={{0,2},{1,3},{2,4},{3,5},{4,6},{5,7},{6,0},{7,1},{8,10},{9,11},{10,... | collective-permute-start | bytes 1437704 | tf_op jit(solution)/shard_map/ppermute | solution.py:32
  7.7 15.3 %collective-permute-start = (bf16[208,1152]{1,0:T(8,128)(2,1)}, bf16[208,1152]{1,0:T(8,128)(2,1)S(1)}, u32[]{:S(2)}, u32[]{:S(2)}) collective-permute-start(bf16[208,1152]{1,0:T(8,128)(2,1)} %get-tuple-element.21), channel_id=1, source_target_pairs={{0,6},{1,7},{2,0},{3,1},{4,2},{5,3},{6,4},{7,5},{8,14},{9,15},{10,... | collective-permute-start | bytes 1437704 | tf_op jit(solution)/shard_map/ppermute | solution.py:32
  9.2 8.9 %collective-permute-start.10 = (bf16[128,1152]{1,0:T(8,128)(2,1)}, bf16[128,1152]{1,0:T(8,128)(2,1)S(1)}, u32[]{:S(2)}, u32[]{:S(2)}) collective-permute-start(bf16[128,1152]{1,0:T(8,128)(2,1)} %get-tuple-element.23), channel_id=1, source_target_pairs={{0,96},{1,97},{2,98},{3,99},{4,100},{5,101},{6,102},{7,103},{8,104... | collective-permute-start | bytes 884744 | tf_op jit(solution)/shard_map/ppermute | solution.py:32
  12.9 8.1 %collective-permute-start.12 = (bf16[128,1152]{1,0:T(8,128)(2,1)}, bf16[128,1152]{1,0:T(8,128)(2,1)S(1)}, u32[]{:S(2)}, u32[]{:S(2)}) collective-permute-start(bf16[128,1152]{1,0:T(8,128)(2,1)} %get-tuple-element.23), channel_id=1, source_target_pairs={{0,32},{1,33},{2,34},{3,35},{4,36},{5,37},{6,38},{7,39},{8,40},{9,... | collective-permute-start | bytes 884744 | tf_op jit(solution)/shard_map/ppermute | solution.py:32
  21.6 11.8 %collective-permute-start.5 = (bf16[208,1152]{1,0:T(8,128)(2,1)S(1)}, bf16[208,1152]{1,0:T(8,128)(2,1)S(1)}, u32[]{:S(2)}, u32[]{:S(2)}) collective-permute-start(bf16[208,1152]{1,0:T(8,128)(2,1)S(1)} %collective-permute-done.2), channel_id=1, source_target_pairs={{0,6},{1,7},{2,0},{3,1},{4,2},{5,3},{6,4},{7,5},{8,14},{9,15},{10,... | collective-permute-start | bytes 1437704 | tf_op jit(solution)/shard_map/ppermute | solution.py:32
  22.8 10.4 %collective-permute-start.3 = (bf16[208,1152]{1,0:T(8,128)(2,1)S(1)}, bf16[208,1152]{1,0:T(8,128)(2,1)S(1)}, u32[]{:S(2)}, u32[]{:S(2)}) collective-permute-start(bf16[208,1152]{1,0:T(8,128)(2,1)S(1)} %collective-permute-done.2), channel_id=1, source_target_pairs={{0,2},{1,3},{2,4},{3,5},{4,6},{5,7},{6,0},{7,1},{8,10},{9,11},{10,... | collective-permute-start | bytes 1437704 | tf_op jit(solution)/shard_map/ppermute | solution.py:32
  26.7 14.4 %collective-permute-start.11 = (bf16[128,1152]{1,0:T(8,128)(2,1)S(1)}, bf16[128,1152]{1,0:T(8,128)(2,1)S(1)}, u32[]{:S(2)}, u32[]{:S(2)}) collective-permute-start(bf16[128,1152]{1,0:T(8,128)(2,1)S(1)} %collective-permute-done.9), channel_id=1, source_target_pairs={{0,96},{1,97},{2,98},{3,99},{4,100},{5,101},{6,102},{7,103},{8,104... | collective-permute-start | bytes 884744 | tf_op jit(solution)/shard_map/ppermute | solution.py:32
  27.5 15.6 %collective-permute-start.13 = (bf16[128,1152]{1,0:T(8,128)(2,1)S(1)}, bf16[128,1152]{1,0:T(8,128)(2,1)S(1)}, u32[]{:S(2)}, u32[]{:S(2)}) collective-permute-start(bf16[128,1152]{1,0:T(8,128)(2,1)S(1)} %collective-permute-done.9), channel_id=1, source_target_pairs={{0,32},{1,33},{2,34},{3,35},{4,36},{5,37},{6,38},{7,39},{8,40},{9,... | collective-permute-start | bytes 884744 | tf_op jit(solution)/shard_map/ppermute | solution.py:32
  33.3 19.6 %collective-permute-start.4 = (bf16[192,1152]{1,0:T(8,128)(2,1)S(1)}, bf16[192,1152]{1,0:T(8,128)(2,1)S(1)}, u32[]{:S(2)}, u32[]{:S(2)}) collective-permute-start(bf16[192,1152]{1,0:T(8,128)(2,1)S(1)} %pad_maximum_fusion.4), channel_id=1, source_target_pairs={{0,2},{1,3},{2,4},{3,5},{4,6},{5,7},{6,0},{7,1},{8,10},{9,11},{10,... | collective-permute-start | bytes 1327112 | tf_op jit(solution)/shard_map/ppermute | solution.py:32
  33.5 20.6 %collective-permute-start.6 = (bf16[224,1152]{1,0:T(8,128)(2,1)S(1)}, bf16[224,1152]{1,0:T(8,128)(2,1)S(1)}, u32[]{:S(2)}, u32[]{:S(2)}) collective-permute-start(bf16[224,1152]{1,0:T(8,128)(2,1)S(1)} %pad_maximum_fusion.3), channel_id=1, source_target_pairs={{0,6},{1,7},{2,0},{3,1},{4,2},{5,3},{6,4},{7,5},{8,14},{9,15},{10,... | collective-permute-start | bytes 1548296 | tf_op jit(solution)/shard_map/ppermute | solution.py:32
  36.3 20.0 %collective-permute-start.7 = (bf16[480,1152]{1,0:T(8,128)(2,1)S(1)}, bf16[480,1152]{1,0:T(8,128)(2,1)S(1)}, u32[]{:S(2)}, u32[]{:S(2)}) collective-permute-start(bf16[480,1152]{1,0:T(8,128)(2,1)S(1)} %slice_dynamic-update-slice_fusion.18.near), channel_id=1, source_target_pairs={{0,8},{1,9},{2,10},{3,11},{4,12},{5,13},{6,14},{7,15},{8,0},{9,1},... | collective-permute-start | bytes 3317768 | tf_op jit(solution)/shard_map/ppermute | solution.py:32
  41.2 8.7 %collective-permute-start.15 = (bf16[128,1152]{1,0:T(8,128)(2,1)S(1)}, bf16[128,1152]{1,0:T(8,128)(2,1)S(1)}, u32[]{:S(2)}, u32[]{:S(2)}) collective-permute-start(bf16[128,1152]{1,0:T(8,128)(2,1)S(1)} %pad_maximum_fusion.6), channel_id=1, source_target_pairs={{0,96},{1,97},{2,98},{3,99},{4,100},{5,101},{6,102},{7,103},{8,104... | collective-permute-start | bytes 884744 | tf_op jit(solution)/shard_map/ppermute | solution.py:32
  43.2 9.6 %collective-permute-start.14 = (bf16[128,1152]{1,0:T(8,128)(2,1)S(1)}, bf16[128,1152]{1,0:T(8,128)(2,1)S(1)}, u32[]{:S(2)}, u32[]{:S(2)}) collective-permute-start(bf16[128,1152]{1,0:T(8,128)(2,1)S(1)} %pad_maximum_fusion.5), channel_id=1, source_target_pairs={{0,32},{1,33},{2,34},{3,35},{4,36},{5,37},{6,38},{7,39},{8,40},{9,... | collective-permute-start | bytes 884744 | tf_op jit(solution)/shard_map/ppermute | solution.py:32
  80.0 14.6 %collective-permute-start.18 = (bf16[640,1152]{1,0:T(8,128)(2,1)S(1)}, bf16[640,1152]{1,0:T(8,128)(2,1)S(1)}, u32[]{:S(2)}, u32[]{:S(2)}) collective-permute-start(bf16[640,1152]{1,0:T(8,128)(2,1)S(1)} %shard_map.78), channel_id=1, source_target_pairs={{0,8},{1,9},{2,10},{3,11},{4,12},{5,13},{6,14},{7,15},{8,0},{9,1},... | collective-permute-start | bytes 4423688 | tf_op jit(solution)/shard_map/ppermute | solution.py:32
  95.7 10.5 %collective-permute-start.22 = (bf16[1024,1152]{1,0:T(8,128)(2,1)}, bf16[1024,1152]{1,0:T(8,128)(2,1)}, u32[]{:S(2)}, u32[]{:S(2)}) collective-permute-start(bf16[1024,1152]{1,0:T(8,128)(2,1)} %fusion.9), channel_id=1, source_target_pairs={{0,8},{1,9},{2,10},{3,11},{4,12},{5,13},{6,14},{7,15},{8,0},{9,1},... | collective-permute-start | bytes 7077896 | tf_op jit(solution)/shard_map/ppermute | solution.py:32
  96.2 29.2 %collective-permute-start.29 = (bf16[512,1152]{1,0:T(8,128)(2,1)}, bf16[512,1152]{1,0:T(8,128)(2,1)S(1)}, u32[]{:S(2)}, u32[]{:S(2)}) collective-permute-start(bf16[512,1152]{1,0:T(8,128)(2,1)} %copy-done.8), channel_id=1, source_target_pairs={{0,1},{1,0},{2,3},{3,2},{4,5},{5,4},{6,7},{7,6},{8,9},{9,8},{10,11... | collective-permute-start | bytes 3538952 | tf_op jit(solution)/shard_map/ppermute | solution.py:32
  101.2 9.7 %collective-permute-start.21 = (bf16[160,1152]{1,0:T(8,128)(2,1)S(1)}, bf16[160,1152]{1,0:T(8,128)(2,1)S(1)}, u32[]{:S(2)}, u32[]{:S(2)}) collective-permute-start(bf16[160,1152]{1,0:T(8,128)(2,1)S(1)} %get-tuple-element.52), channel_id=1, source_target_pairs={{0,6},{1,7},{2,0},{3,1},{4,2},{5,3},{6,4},{7,5},{8,14},{9,15},{10,... | collective-permute-start | bytes 1105928 | tf_op jit(solution)/shard_map/ppermute | solution.py:32
  101.3 18.9 %collective-permute-start.20 = (bf16[160,1152]{1,0:T(8,128)(2,1)S(1)}, bf16[160,1152]{1,0:T(8,128)(2,1)S(1)}, u32[]{:S(2)}, u32[]{:S(2)}) collective-permute-start(bf16[160,1152]{1,0:T(8,128)(2,1)S(1)} %get-tuple-element.53), channel_id=1, source_target_pairs={{0,2},{1,3},{2,4},{3,5},{4,6},{5,7},{6,0},{7,1},{8,10},{9,11},{10,... | collective-permute-start | bytes 1105928 | tf_op jit(solution)/shard_map/ppermute | solution.py:32
  102.8 17.4 %collective-permute-start.19 = (bf16[160,1152]{1,0:T(8,128)(2,1)S(1)}, bf16[160,1152]{1,0:T(8,128)(2,1)S(1)}, u32[]{:S(2)}, u32[]{:S(2)}) collective-permute-start(bf16[160,1152]{1,0:T(8,128)(2,1)S(1)} %get-tuple-element.51), channel_id=1, source_target_pairs={{0,4},{1,5},{2,6},{3,7},{4,0},{5,1},{6,2},{7,3},{8,12},{9,13},{10,... | collective-permute-start | bytes 1105928 | tf_op jit(solution)/shard_map/ppermute | solution.py:32
  108.7 11.8 %collective-permute-start.24 = (bf16[128,1152]{1,0:T(8,128)(2,1)S(1)}, bf16[128,1152]{1,0:T(8,128)(2,1)S(1)}, u32[]{:S(2)}, u32[]{:S(2)}) collective-permute-start(bf16[128,1152]{1,0:T(8,128)(2,1)S(1)} %get-tuple-element.46), channel_id=1, source_target_pairs={{0,96},{1,97},{2,98},{3,99},{4,100},{5,101},{6,102},{7,103},{8,104... | collective-permute-start | bytes 884744 | tf_op jit(solution)/shard_map/ppermute | solution.py:32
  111.0 9.5 %collective-permute-start.23 = (bf16[128,1152]{1,0:T(8,128)(2,1)S(1)}, bf16[128,1152]{1,0:T(8,128)(2,1)S(1)}, u32[]{:S(2)}, u32[]{:S(2)}) collective-permute-start(bf16[128,1152]{1,0:T(8,128)(2,1)S(1)} %get-tuple-element.48), channel_id=1, source_target_pairs={{0,32},{1,33},{2,34},{3,35},{4,36},{5,37},{6,38},{7,39},{8,40},{9,... | collective-permute-start | bytes 884744 | tf_op jit(solution)/shard_map/ppermute | solution.py:32
  120.7 20.3 %collective-permute-start.26 = (bf16[256,1152]{1,0:T(8,128)(2,1)S(1)}, bf16[256,1152]{1,0:T(8,128)(2,1)S(1)}, u32[]{:S(2)}, u32[]{:S(2)}) collective-permute-start(bf16[256,1152]{1,0:T(8,128)(2,1)S(1)} %get-tuple-element.32), channel_id=1, source_target_pairs={{0,96},{1,97},{2,98},{3,99},{4,100},{5,101},{6,102},{7,103},{8,104... | collective-permute-start | bytes 1769480 | tf_op jit(solution)/shard_map/ppermute | solution.py:32
  120.8 20.2 %collective-permute-start.25 = (bf16[256,1152]{1,0:T(8,128)(2,1)S(1)}, bf16[256,1152]{1,0:T(8,128)(2,1)S(1)}, u32[]{:S(2)}, u32[]{:S(2)}) collective-permute-start(bf16[256,1152]{1,0:T(8,128)(2,1)S(1)} %get-tuple-element.31), channel_id=1, source_target_pairs={{0,32},{1,33},{2,34},{3,35},{4,36},{5,37},{6,38},{7,39},{8,40},{9,... | collective-permute-start | bytes 1769480 | tf_op jit(solution)/shard_map/ppermute | solution.py:32
  122.3 6.0 %collective-permute-start.27 = (bf16[80,1152]{1,0:T(8,128)(2,1)S(1)}, bf16[80,1152]{1,0:T(8,128)(2,1)S(1)}, u32[]{:S(2)}, u32[]{:S(2)}) collective-permute-start(bf16[80,1152]{1,0:T(8,128)(2,1)S(1)} %slice.373), channel_id=1, source_target_pairs={{0,1},{1,0},{2,3},{3,2},{4,5},{5,4},{6,7},{7,6},{8,9},{9,8},{10,11... | collective-permute-start | bytes 552968 | tf_op jit(solution)/shard_map/ppermute | solution.py:32
  125.7 7.6 %collective-permute-start.32 = (bf16[128,1152]{1,0:T(8,128)(2,1)S(1)}, bf16[128,1152]{1,0:T(8,128)(2,1)S(1)}, u32[]{:S(2)}, u32[]{:S(2)}) collective-permute-start(bf16[128,1152]{1,0:T(8,128)(2,1)S(1)} %get-tuple-element.55), channel_id=1, source_target_pairs={{0,6},{1,7},{2,0},{3,1},{4,2},{5,3},{6,4},{7,5},{8,14},{9,15},{10,... | collective-permute-start | bytes 884744 | tf_op jit(solution)/shard_map/ppermute | solution.py:32
  125.8 15.0 %collective-permute-start.31 = (bf16[128,1152]{1,0:T(8,128)(2,1)S(1)}, bf16[128,1152]{1,0:T(8,128)(2,1)S(1)}, u32[]{:S(2)}, u32[]{:S(2)}) collective-permute-start(bf16[128,1152]{1,0:T(8,128)(2,1)S(1)} %get-tuple-element.56), channel_id=1, source_target_pairs={{0,2},{1,3},{2,4},{3,5},{4,6},{5,7},{6,0},{7,1},{8,10},{9,11},{10,... | collective-permute-start | bytes 884744 | tf_op jit(solution)/shard_map/ppermute | solution.py:32
  128.3 12.5 %collective-permute-start.30 = (bf16[128,1152]{1,0:T(8,128)(2,1)S(1)}, bf16[128,1152]{1,0:T(8,128)(2,1)S(1)}, u32[]{:S(2)}, u32[]{:S(2)}) collective-permute-start(bf16[128,1152]{1,0:T(8,128)(2,1)S(1)} %get-tuple-element.54), channel_id=1, source_target_pairs={{0,4},{1,5},{2,6},{3,7},{4,0},{5,1},{6,2},{7,3},{8,12},{9,13},{10,... | collective-permute-start | bytes 884744 | tf_op jit(solution)/shard_map/ppermute | solution.py:32
  133.3 7.7 %collective-permute-start.28 = (bf16[80,1152]{1,0:T(8,128)(2,1)S(1)}, bf16[80,1152]{1,0:T(8,128)(2,1)S(1)}, u32[]{:S(2)}, u32[]{:S(2)}) collective-permute-start(bf16[80,1152]{1,0:T(8,128)(2,1)S(1)} %add_convert_fusion.4), channel_id=1, source_target_pairs={{0,16},{1,17},{2,18},{3,19},{4,20},{5,21},{6,22},{7,23},{8,24},{9,... | collective-permute-start | bytes 552968 | tf_op jit(solution)/shard_map/ppermute | solution.py:32
  141.4 6.0 %collective-permute-start.35 = (bf16[80,1152]{1,0:T(8,128)(2,1)S(1)}, bf16[80,1152]{1,0:T(8,128)(2,1)S(1)}, u32[]{:S(2)}, u32[]{:S(2)}) collective-permute-start(bf16[80,1152]{1,0:T(8,128)(2,1)S(1)} %add_convert_fusion.3), channel_id=1, source_target_pairs={{0,32},{1,33},{2,34},{3,35},{4,36},{5,37},{6,38},{7,39},{8,40},{9,... | collective-permute-start | bytes 552968 | tf_op jit(solution)/shard_map/ppermute | solution.py:32
  142.9 7.5 %collective-permute-start.34 = (bf16[80,1152]{1,0:T(8,128)(2,1)S(1)}, bf16[80,1152]{1,0:T(8,128)(2,1)S(1)}, u32[]{:S(2)}, u32[]{:S(2)}) collective-permute-start(bf16[80,1152]{1,0:T(8,128)(2,1)S(1)} %add_convert_fusion.3), channel_id=1, source_target_pairs={{0,64},{1,65},{2,66},{3,67},{4,68},{5,69},{6,70},{7,71},{8,72},{9,... | collective-permute-start | bytes 552968 | tf_op jit(solution)/shard_map/ppermute | solution.py:32
  142.9 11.2 %collective-permute-start.33 = (bf16[128,1152]{1,0:T(8,128)(2,1)S(1)}, bf16[128,1152]{1,0:T(8,128)(2,1)S(1)}, u32[]{:S(2)}, u32[]{:S(2)}) collective-permute-start(bf16[128,1152]{1,0:T(8,128)(2,1)S(1)} %slice.372), channel_id=1, source_target_pairs={{0,16},{1,17},{2,18},{3,19},{4,20},{5,21},{6,22},{7,23},{8,24},{9,... | collective-permute-start | bytes 884744 | tf_op jit(solution)/shard_map/ppermute | solution.py:32
  (24 other events, 166.4 us)
